TPU v7x, 256 devices: a whole 4x4x8 slice. The times are simulated.
256 devices in a mesh: section: 2 (over core), mp: 8 (over z), dp: 16 (over y, x).
Axes of the slice: x: 4, y: 4, z: 8, core: 2. Of those that a mesh axis runs over, the one named last changes fastest.
Arguments:
- patches: bfloat16 [16, 256, 6144], P('dp', ('section', 'mp')), may hold values from -6 to 6
- vis_index: int32 [16, 256], P('dp', ('section', 'mp')), may hold values from 0 to 1023, as said below
- input_weight: bfloat16 [6144, 3, 3072], P('section', None, 'mp'), may hold values from -0.078125 to 0.078125
- output_weight: bfloat16 [3072, 6144], P('mp', 'section'), may hold values from -1.75 to 1.75
- embed_weight: bfloat16 [6144, 512], P(('section', 'mp')), may hold values from -0.078125 to 0.078125
- mask_token: bfloat16 [512], replicated, may hold values from -5 to 5
- position_table: bfloat16 [1024, 512], P(('section', 'mp')), may hold values from -5 to 5
- decoder_input: bfloat16 [512, 3, 512], replicated, may hold values from -0.25 to 0.25
- decoder_output: bfloat16 [512, 512], replicated, may hold values from -0.25 to 0.25
- pixel_weight: bfloat16 [512, 768], replicated, may hold values from -0.25 to 0.25
- target: bfloat16 [16, 1024, 768], P('dp', ('section', 'mp')), may hold values from -6 to 6
Outputs:
- prediction: bfloat16 [16, 1024, 768], P('dp', ('section', 'mp'))
- patch_grad: bfloat16 [16, 256, 6144], P('dp', ('section', 'mp'))
Inputs may be any that keep to these rules, and one draw needn't show every extreme that they name: `vis_index`: in each scene the 256 positions are distinct. Split a scene's visible patches into 16 aligned blocks of 16 and the positions into 16 aligned ranges of 64: each block has exactly 2 patches in a quarter of the ranges (rounded down), none in another quarter and 1 in each other range.
All inputs are finite; a program needn't handle non-finite values.
Results may differ from a plain program's by a relative error of at most 0.03.
Values may be sent and summed in bfloat16 or wider, within the bound.
No kernel may reach another device: no remote copies, remote signals or barrier semaphores. Data moves between devices by JAX's collectives and lax.ppermute only.
A program may use at most 128 MiB of HBM per device.

v0:
```python
import math

import jax
import jax.numpy as jnp
from jax import lax
from jax.experimental import pallas as pl
from jax.experimental.pallas import tpu as pltpu
from jax.sharding import PartitionSpec as P

HD = 128
DHEADS = 16
DHD = 32
EPSILON = 1e-06
LOG2E = math.log2(math.e)
F32 = jnp.float32
BF16 = jnp.bfloat16
OFFSETS = (0, -1, 1, -2, 2, -3, 3, -4)


def dot(a, b):
    return lax.dot_general(a, b, (((1,), (0,)), ((), ())), preferred_element_type=F32)


def dot_nt(a, b):
    return lax.dot_general(a, b, (((1,), (1,)), ((), ())), preferred_element_type=F32)


def dot_tn(a, b):
    return lax.dot_general(a, b, (((0,), (0,)), ((), ())), preferred_element_type=F32)


def row_norm(values, axis=-1):
    centre = jnp.mean(values, axis=axis, keepdims=True)
    centered = values - centre
    inverse = lax.rsqrt(jnp.mean(centered * centered, axis=axis, keepdims=True) + EPSILON)
    return centered * inverse, inverse


def norm_back(normed, inverse, gradient, axis=-1):
    mean_grad = jnp.mean(gradient, axis=axis, keepdims=True)
    mean_dot = jnp.mean(gradient * normed, axis=axis, keepdims=True)
    return inverse * (gradient - mean_grad - normed * mean_dot)


def lanes(columns, rows):
    lane = lax.broadcasted_iota(jnp.int32, (rows, 128), 1)
    out = jnp.zeros((rows, 128), F32)
    for at, column in enumerate(columns):
        out = jnp.where(lane == at, column, out)
    return out


def call(kernel, out_shape, *args, scratch=(), far=(), limit=24):
    specs = [pl.BlockSpec(memory_space=pltpu.SMEM)]
    for at in range(1, len(args)):
        specs.append(pl.BlockSpec(memory_space=pl.ANY if at in far else pltpu.VMEM))
    return pl.pallas_call(
        kernel,
        out_shape=out_shape,
        in_specs=specs,
        out_specs=jax.tree.map(lambda _: pl.BlockSpec(memory_space=pltpu.VMEM), out_shape),
        scratch_shapes=list(scratch),
        compiler_params=pltpu.CompilerParams(vmem_limit_bytes=limit * 2**20),
    )(*args)


def sds(shape, dtype):
    return jax.ShapeDtypeStruct(shape, dtype)


def fetch(w, held, sems):
    copies = [pltpu.make_async_copy(w.at[at], held.at[at], sems.at[at]) for at in range(3)]
    for copy in copies:
        copy.start()
    return copies


def fold_kernel(ids, pieces, wo, out, out_low):
    slab = wo.shape[1] // 8
    total = dot_nt(pieces[0], wo[:, :slab])
    for at in range(1, 8):
        total = total + dot_nt(pieces[at], wo[:, at * slab : (at + 1) * slab])
    out[...] = total
    out_low[...] = total.astype(BF16)


def project_kernel(ids, *refs):
    chunks = refs[:8]
    w, we = refs[8:10]
    x_out, p_own, p_send, stats, xp_own, xp_send = refs[10:16]
    xc, held, sems = refs[16:]
    copies = fetch(w, held, sems)
    half = held.shape[1]
    width = held.shape[2]
    slab = half // 8
    tok = x_out.shape[2]
    group = 8 * tok
    m = ids[1]
    for chunk, offset in zip(chunks, OFFSETS):
        at = lax.rem(m + offset + 8, 8)
        value = chunk[...]
        x_out[0, at] = value[:tok]
        x_out[1, at] = value[tok:]
        wide = value.astype(F32)
        centre = jnp.mean(wide, axis=1, keepdims=True)
        centered = wide - centre
        spread = jnp.sum(centered * centered, axis=1, keepdims=True)
        low = centered.astype(BF16)
        both = lanes((centre, spread), 2 * tok)
        row = pl.multiple_of(at * tok, tok)
        xc[pl.ds(row, tok), :] = low[:tok]
        xc[pl.ds(row + group, tok), :] = low[tok:]
        stats[pl.ds(row, tok), :] = both[:tok]
        stats[pl.ds(row + group, tok), :] = both[tok:]
    xc[2 * group :, :] = jnp.ones((16, half), BF16)
    for at in range(3):
        copies[at].wait()
        product = dot(xc[...], held[at])
        p_own[:, at * width : (at + 1) * width] = product
        p_send[:, at * width : (at + 1) * width] = product.astype(BF16)
    column = pl.multiple_of(m * slab, 128)
    raw = jnp.concatenate(
        [x_out[0, :, :, pl.ds(column, slab)], x_out[1, :, :, pl.ds(column, slab)]]
    ).reshape(2 * group, slab)
    part = dot(raw, we[...])
    xp_own[...] = part[:group]
    xp_send[...] = part[group:].astype(BF16)


def attend_kernel(ids, p_own, p_other, st_own, st_other, att, e_out, q_out, k_out, v_out, aux):
    rows = st_own.shape[0]
    group = rows // 2
    width = p_own.shape[1] // 3
    heads = width // HD
    model = 2 * 8 * width
    stats_other = jnp.concatenate([st_other[group:, :], st_other[:group, :]])
    m_own, s_own = st_own[:, 0:1], st_own[:, 1:2]
    m_other, s_other = stats_other[:, 0:1], stats_other[:, 1:2]
    gap = (m_own - m_other) * 0.5
    centre = (m_own + m_other) * 0.5
    inverse = lax.rsqrt((s_own + s_other) / model + gap * gap + EPSILON)
    slope = p_own[rows : rows + 1, :] - p_other[rows : rows + 1, :].astype(F32)
    columns = [centre, inverse]
    inv_q, inv_k, inv_l = [], [], []
    factor = LOG2E * HD**-0.5

    def mixture(at):
        cols = slice(at * HD, (at + 1) * HD)
        other = jnp.concatenate([p_other[group:rows, cols], p_other[:group, cols]]).astype(F32)
        return inverse * (p_own[:rows, cols] + other + gap * slope[:, cols])

    for head in range(heads):
        cols = slice(head * HD, (head + 1) * HD)
        q_hat, q_inv = row_norm(mixture(head))
        k_hat, k_inv = row_norm(mixture(heads + head))
        v_low = mixture(2 * heads + head).astype(BF16)
        e = jnp.exp2(dot_nt(q_hat.astype(BF16), k_hat.astype(BF16)) * factor)
        l_inv = 1.0 / jnp.sum(e, axis=1, keepdims=True)
        e_low = e.astype(BF16)
        att[:, cols] = (dot(e_low[:group], v_low) * l_inv[:group]).astype(BF16)
        e_out[head] = e_low
        q_out[:, cols] = q_hat
        k_out[:, cols] = k_hat
        v_out[:, cols] = v_low
        inv_q.append(q_inv)
        inv_k.append(k_inv)
        inv_l.append(l_inv)
    aux[...] = lanes(columns + inv_l + inv_q + inv_k, rows)


def feature_parts(rows, gm, glayer, x_rows, centre, inverse, held, m, store):
    half, width = held.shape[1:]
    slab = half // 8
    total = jnp.zeros((rows, 1), F32)
    total_dot = jnp.zeros((rows, 1), F32)
    for block in range(8):
        cols = slice(block * slab, (block + 1) * slab)
        g = dot_nt(gm[:, :width], held[0, cols, :])
        g = g + dot_nt(gm[:, width : 2 * width], held[1, cols, :])
        g = g + dot_nt(gm[:, 2 * width :], held[2, cols, :])
        normed = (x_rows(cols).astype(F32) - centre) * inverse
        total = total + jnp.sum(g, axis=1, keepdims=True)
        total_dot = total_dot + jnp.sum(g * normed, axis=1, keepdims=True)
        mine = jnp.where(block == m, 1.0, 0.0)
        store(cols, (g * inverse + glayer * mine).astype(BF16))
    store(slice(half, half + 128), lanes((total, total_dot), rows).astype(BF16))


def encoder_back_kernel(
    ids, g_own, g_other, wpt, e_in, q_in, k_in, v_in, aux, x_in, w, we, first, gmix, glayer_out, few, held, sems
):
    copies = fetch(w, held, sems)
    rows = q_in.shape[0]
    width = q_in.shape[1]
    heads = width // HD
    tok = x_in.shape[2]
    group = 8 * tok
    m = ids[1]
    factor = HD**-0.5
    gemb = jnp.concatenate([g_own[...], g_other[...]])
    gatt = dot(gemb, wpt[...]).astype(BF16)
    for head in range(heads):
        cols = slice(head * HD, (head + 1) * HD)
        g_head = gatt[:, cols]
        q_hat, k_hat, v_low = q_in[:, cols], k_in[:, cols], v_in[:, cols]
        l_inv = aux[:, 2 + head : 3 + head]
        q_inv = aux[:, 2 + heads + head : 3 + heads + head]
        k_inv = aux[:, 2 + 2 * heads + head : 3 + 2 * heads + head]
        p = e_in[head].astype(F32) * l_inv
        gp = dot_nt(g_head, v_low)
        delta = jnp.sum(p * gp, axis=1, keepdims=True)
        gs = (p * (gp - delta)).astype(BF16)
        gq = dot(gs, k_hat.astype(BF16)) * factor
        gk = dot_tn(gs, q_hat.astype(BF16)) * factor
        gv = dot_tn(p.astype(BF16), g_head)
        gmix[:, head * HD : (head + 1) * HD] = norm_back(q_hat, q_inv, gq).astype(BF16)
        gmix[:, width + head * HD : width + (head + 1) * HD] = norm_back(k_hat, k_inv, gk).astype(BF16)
        gmix[:, 2 * width + head * HD : 2 * width + (head + 1) * HD] = gv.astype(BF16)
    glayer_out[...] = dot_nt(gemb, we[...])
    ats = [lax.rem(m + 4, 8), lax.rem(m + 5, 8)]
    blocks = [(rel, at) for at in ats for rel in range(2)]

    def rows_of(ref):
        return jnp.concatenate(
            [ref[pl.ds(pl.multiple_of(at * tok, tok) + rel * group, tok), :] for rel, at in blocks]
        )

    few[...] = rows_of(gmix)
    some = rows_of(aux)

    def x_rows(cols):
        return jnp.concatenate([x_in[rel, at, :, cols] for rel, at in blocks])

    def store(cols, value):
        first[:, cols] = value

    for copy in copies:
        copy.wait()
    feature_parts(4 * tok, few[...], rows_of(glayer_out), x_rows, some[:, 0:1], some[:, 1:2], held, m, store)


def feature_kernel(ids, gmix, glayer, aux, x_in, w, out, held, sems):
    copies = fetch(w, held, sems)
    tok = x_in.shape[2]
    rows = gmix.shape[0]

    def x_rows(cols):
        return x_in[:, :, :, cols].reshape(rows, cols.stop - cols.start)

    def store(cols, value):
        value = value.reshape(2, 8, tok, cols.stop - cols.start)
        out[:, :tok, cols] = value[0]
        out[:, tok:, cols] = value[1]

    for copy in copies:
        copy.wait()
    feature_parts(rows, gmix[...], glayer[...], x_rows, aux[:, 0:1], aux[:, 1:2], held, ids[1], store)


def final_kernel(ids, own, other, x_own, out):
    s = ids[0]
    half = x_own.shape[1] // 2
    model = x_own.shape[1]
    normed, inverse = row_norm(x_own[...].astype(F32))
    mine, theirs = own[...], other[...].astype(F32)
    total = (mine[:, half : half + 1] + theirs[:, half : half + 1]) / model
    total_dot = (mine[:, half + 1 : half + 2] + theirs[:, half + 1 : half + 2]) / model
    first = jnp.where(s == 0, mine[:, :half], theirs[:, :half])
    second = jnp.where(s == 0, theirs[:, :half], mine[:, :half])
    out[:, :half] = (first - inverse * (total + normed[:, :half] * total_dot)).astype(BF16)
    out[:, half:] = (second - inverse * (total + normed[:, half:] * total_dot)).astype(BF16)


def head_norm_t(values):
    width, n = values.shape
    hat, inverse = row_norm(values.reshape(DHEADS, DHD, n), axis=1)
    return hat.reshape(width, n), inverse


def head_back_t(hat, inverse, gradient):
    width, n = hat.shape
    back = norm_back(
        hat.reshape(DHEADS, DHD, n), inverse, gradient.reshape(DHEADS, DHD, n), axis=1
    )
    return back.reshape(width, n)


def mask_kernel(ids, table, mask, w, pos_vis, vis_row, hidden, k_t, v, wq_t, wk_t):
    members, pos_dev = table.shape[0], table.shape[1] - 16
    npos, width = members * pos_dev, table.shape[2]
    nvis = vis_row.shape[1]
    pos_all = table[:, :pos_dev, :].reshape(npos, width)
    codes = jnp.sum(table[:, pos_dev:, :].astype(F32), axis=0)
    row = codes[0:1, :nvis] * 32.0 + codes[1:2, :nvis]
    other = jnp.concatenate([row[:, nvis // 2 :], row[:, : nvis // 2]], axis=1)
    vis = jnp.where(ids[0] == 0, row, other).astype(jnp.int32)
    vis_row[...] = vis
    hot = jnp.where(lax.broadcasted_iota(jnp.int32, (npos, nvis), 0) == vis, 1.0, 0.0).astype(BF16)
    pos_vis[...] = dot_tn(hot, pos_all)
    hidden[...] = 1.0 - dot_nt(jnp.ones((16, nvis), BF16), hot)[0:1, :]
    hat, _ = row_norm(pos_all.astype(F32) + mask[...].astype(F32))
    low = hat.astype(BF16)
    wq_t[...] = w[0].T
    wk_t[...] = w[1].T
    key_hat, _ = head_norm_t(dot_nt(wk_t[...], low))
    k_t[...] = key_hat.astype(BF16)
    v[...] = dot(low, w[2]).astype(BF16)


def decoder_kernel(
    ids, vis_row, emb_own, emb_other, pos_vis, hidden, km_t, vm, pos_own, mask, wq_t, wk_t, w, w_out, w_pix, target,
    pred, g_own, g_other, em_ref, ev_ref,
):
    npos_dev, width = pos_own.shape
    nvis = pos_vis.shape[0]
    group = nvis // 2
    member = ids[2]
    groups = width // 128
    per = 128 // DHD
    rows = per * npos_dev
    factor = DHD**-0.5
    emb = jnp.concatenate([emb_own[...], emb_other[...]])
    vis_hat, vis_inv = row_norm(emb.astype(F32) + pos_vis[...])
    vis_low = vis_hat.astype(BF16)
    kv_hat, kv_inv = head_norm_t(dot_nt(wk_t[...], vis_low))
    kv_t = kv_hat.astype(BF16)
    vv = dot(vis_low, w[2]).astype(BF16)
    position = lax.broadcasted_iota(jnp.int32, (npos_dev, nvis), 0) + member * npos_dev
    hot = jnp.where(position == vis_row[...], 1.0, 0.0)
    seen = jnp.sum(hot, axis=1, keepdims=True)
    hot_low = hot.astype(BF16)
    filled = dot(hot_low, emb) + (1.0 - seen) * mask[...].astype(F32)
    stream = filled + pos_own[...].astype(F32)
    own_hat, own_inv = row_norm(stream)
    q_t, q_inv = head_norm_t(dot_nt(wq_t[...], own_hat.astype(BF16)))
    q_low = q_t.T.astype(BF16)
    head_mask = (
        lax.broadcasted_iota(jnp.int32, (rows, 128), 0) // npos_dev
        == lax.broadcasted_iota(jnp.int32, (rows, 128), 1) // DHD
    )

    def spread(values):
        return jnp.where(head_mask, jnp.concatenate([values] * per, axis=0), jnp.zeros((), values.dtype))

    def gather(values):
        return jnp.sum(jnp.where(head_mask, values, 0.0).reshape(per, npos_dev, 128), axis=0)

    attended, inv_l = [], []
    for at in range(groups):
        cols = slice(at * 128, (at + 1) * 128)
        q_wide = spread(q_low[:, cols])
        em = jnp.exp2(dot(q_wide, km_t[cols, :]) * (factor * LOG2E)) * hidden[...]
        ev = jnp.exp2(dot(q_wide, kv_t[cols, :]) * (factor * LOG2E))
        l_inv = 1.0 / (jnp.sum(em, axis=1, keepdims=True) + jnp.sum(ev, axis=1, keepdims=True))
        em_low, ev_low = em.astype(BF16), ev.astype(BF16)
        em_ref[at] = em_low
        ev_ref[at] = ev_low
        attended.append(gather((dot(em_low, vm[:, cols]) + dot(ev_low, vv[:, cols])) * l_inv))
        inv_l.append(l_inv)
    att = jnp.concatenate(attended, axis=1)
    second = stream + dot(att.astype(BF16), w_out[...])
    final_hat, final_inv = row_norm(second)
    full = dot(final_hat.astype(BF16), w_pix[...])
    pred[...] = full.astype(BF16)
    error = jnp.where(seen > 0, 0.0, full - target[...].astype(F32)).astype(BF16)
    g_second = norm_back(final_hat, final_inv, dot_nt(error, w_pix[...]))
    g_att = dot_nt(g_second.astype(BF16), w_out[...]).astype(BF16)
    product = g_att.astype(F32) * att
    gq, gk_t, gv = [], [], []
    for at in range(groups):
        cols = slice(at * 128, (at + 1) * 128)
        q_wide = spread(q_low[:, cols])
        g_wide = spread(g_att[:, cols])
        delta = jnp.sum(spread(product[:, cols]), axis=1, keepdims=True)
        l_inv = inv_l[at]
        pv = ev_ref[at].astype(F32) * l_inv
        gs_v = (pv * (dot_nt(g_wide, vv[:, cols]) - delta)).astype(BF16)
        pm = em_ref[at].astype(F32) * l_inv
        gs_m = (pm * (dot_nt(g_wide, vm[:, cols]) - delta)).astype(BF16)
        gq.append(gather(dot_nt(gs_m, km_t[cols, :]) + dot_nt(gs_v, kv_t[cols, :])) * factor)
        gk_t.append(dot_tn(q_wide, gs_v) * factor)
        gv.append(dot_tn(pv.astype(BF16), g_wide).astype(BF16))
    gq_back = head_back_t(q_t, q_inv, jnp.concatenate(gq, axis=1).T).T.astype(BF16)
    g_stream_own = g_second + norm_back(own_hat, own_inv, dot_nt(gq_back, w[0]))
    gk_back = head_back_t(kv_hat, kv_inv, jnp.concatenate(gk_t, axis=0)).T.astype(BF16)
    from_keys = dot_nt(gk_back, w[1]) + dot_nt(jnp.concatenate(gv, axis=1), w[2])
    part = norm_back(vis_hat, vis_inv, from_keys) + dot_tn(hot_low, g_stream_own.astype(BF16))
    g_own[...] = part[:group]
    g_other[...] = part[group:].astype(BF16)


def shards(
    patches,
    vis_index,
    input_weight,
    output_weight,
    embed_weight,
    mask_token,
    position_table,
    decoder_input,
    decoder_output,
    pixel_weight,
    target,
):
    section = lax.axis_index("section")
    column = lax.axis_index("mp")
    member = lax.axis_index(("section", "mp"))
    copies = lax.axis_size("dp")
    ids = jnp.stack([section, column, member]).astype(jnp.int32)
    x_own = patches[0]
    tok, model = x_own.shape
    half = model // 2
    slab, dec_width = embed_weight.shape
    width = output_weight.shape[0]
    heads = width // HD
    group = 8 * tok
    nvis = 2 * group
    pos_dev = position_table.shape[0]
    npos = 16 * pos_dev

    def swap(value):
        return lax.ppermute(value, "section", [(0, 1), (1, 0)])

    def shift(value, by):
        return lax.ppermute(value, "mp", [(i, (i + by) % 8) for i in range(8)])

    def exchange(value, axis):
        return lax.all_to_all(value, axis, 0, 0, tiled=True)

    spread = 4 if copies % 4 == 0 else 1
    dec_cols = dec_width // spread
    place = lax.axis_index("dp") % spread
    pieces = lax.all_gather(
        lax.dynamic_slice_in_dim(embed_weight, place * dec_cols, dec_cols, 1).T, "mp", axis=0, tiled=False
    )

    mine = lax.dynamic_slice_in_dim(x_own, section * half, half, 1)
    theirs = swap(lax.dynamic_slice_in_dim(x_own, (1 - section) * half, half, 1))
    chunk = jnp.concatenate([mine, theirs])
    chunks = {0: chunk}
    right = left = chunk
    for step in range(1, 5):
        right = shift(right, 1)
        chunks[-step] = right
        if step < 4:
            left = shift(left, -1)
            chunks[step] = left

    index, _, _ = lax.optimization_barrier((vis_index[0], chunks[-1], pieces))
    row = jnp.zeros((nvis,), jnp.int32)
    row = lax.dynamic_update_slice_in_dim(row, index, member * tok, 0)
    codes = jnp.pad(jnp.stack([row // 32, row % 32]), ((0, 14), (0, dec_width - nvis)))
    table = jnp.concatenate([position_table, codes.astype(BF16)])
    table = lax.all_gather(table, ("section", "mp"), axis=0, tiled=False)

    w_in = input_weight.transpose(1, 0, 2)
    held = (pltpu.VMEM(w_in.shape, BF16), pltpu.SemaphoreType.DMA((3,)))
    wp_part, wp_send = call(
        fold_kernel, (sds((dec_cols, width), F32), sds((dec_cols, width), BF16)), ids, pieces, output_weight
    )
    x_all, p_own, p_send, stats, xp_own, xp_send = call(
        project_kernel,
        (
            sds((2, 8, tok, half), BF16),
            sds((nvis + 16, 3 * width), F32),
            sds((nvis + 16, 3 * width), BF16),
            sds((nvis, 128), F32),
            sds((group, dec_width), F32),
            sds((group, dec_width), BF16),
        ),
        ids,
        *[chunks[offset] for offset in OFFSETS],
        w_in,
        embed_weight,
        scratch=(pltpu.VMEM((nvis + 16, half), BF16),) + held,
        far=(9,),
    )
    p_other = swap(p_send)
    stats_other = swap(stats)
    wp_piece = (wp_part + swap(wp_send).astype(F32)).astype(BF16)
    wpt = lax.all_to_all(
        jnp.broadcast_to(wp_piece, (spread, dec_cols, width)),
        "dp",
        0,
        0,
        tiled=True,
        axis_index_groups=[[y * spread + x for x in range(spread)] for y in range(copies // spread)],
    ).reshape(dec_width, width)
    xp_other = swap(xp_send)

    att, e_enc, q_enc, k_enc, v_enc, aux = call(
        attend_kernel,
        (
            sds((group, width), BF16),
            sds((heads, nvis, nvis), BF16),
            sds((nvis, width), F32),
            sds((nvis, width), F32),
            sds((nvis, width), BF16),
            sds((nvis, 128), F32),
        ),
        ids,
        p_own,
        p_other,
        stats,
        stats_other,
    )
    embed_part = dot_nt(att, wpt) + xp_own + xp_other.astype(F32)

    def reduce_and_gather(part):
        received = exchange(part.astype(BF16).reshape(8, tok, dec_width), "mp")
        total = jnp.sum(received.astype(F32), axis=0).astype(BF16)
        gathered = exchange(jnp.broadcast_to(total, (8, tok, dec_width)), "mp").reshape(group, dec_width)
        return gathered, swap(gathered)

    w_dec = decoder_input.transpose(1, 0, 2)
    mask_row = mask_token.reshape(1, dec_width)
    table, embed_part = lax.optimization_barrier((table, embed_part))
    pos_vis, vis_row, hidden, km_t, vm, wq_t, wk_t = call(
        mask_kernel,
        (
            sds((nvis, dec_width), F32),
            sds((1, nvis), jnp.int32),
            sds((1, npos), F32),
            sds((dec_width, npos), BF16),
            sds((npos, dec_width), BF16),
            sds((dec_width, dec_width), BF16),
            sds((dec_width, dec_width), BF16),
        ),
        ids,
        table,
        mask_row,
        w_dec,
    )
    emb_own, emb_other = reduce_and_gather(embed_part)

    groups = dec_width // 128
    rows = (128 // DHD) * pos_dev
    prediction, g_own, g_send = call(
        decoder_kernel,
        (
            sds((pos_dev, target.shape[2]), BF16),
            sds((group, dec_width), F32),
            sds((group, dec_width), BF16),
        ),
        ids,
        vis_row,
        emb_own,
        emb_other,
        pos_vis,
        hidden,
        km_t,
        vm,
        position_table,
        mask_row,
        wq_t,
        wk_t,
        w_dec,
        decoder_output,
        pixel_weight,
        target[0],
        scratch=(pltpu.VMEM((groups, rows, npos), BF16), pltpu.VMEM((groups, rows, nvis), BF16)),
    )
    ge_own, ge_other = reduce_and_gather(g_own + swap(g_send).astype(F32))

    first, gmix, glayer = call(
        encoder_back_kernel,
        (
            sds((4 * tok, half + 128), BF16),
            sds((nvis, 3 * width), BF16),
            sds((nvis, slab), F32),
        ),
        ids,
        ge_own,
        ge_other,
        wpt,
        e_enc,
        q_enc,
        k_enc,
        v_enc,
        aux,
        x_all,
        w_in,
        embed_weight,
        scratch=(pltpu.VMEM((4 * tok, 3 * width), BF16),) + held,
        far=(10,),
    )
    parts = call(
        feature_kernel,
        sds((8, 2 * tok, half + 128), BF16),
        ids,
        gmix,
        glayer,
        aux,
        x_all,
        w_in,
        scratch=held,
        far=(5,),
    )

    def part(offset):
        return lax.dynamic_index_in_dim(parts, (column + offset) % 8, 0, False).astype(F32)

    right, left = first[: 2 * tok], first[2 * tok :]
    for step in range(3):
        moved_right, moved_left = shift(right, 1), shift(left, -1)
        right = (moved_right.astype(F32) + part(3 - step)).astype(BF16)
        if step < 2:
            left = (moved_left.astype(F32) + part(-2 + step)).astype(BF16)
    total = shift(right, 1).astype(F32) + moved_left.astype(F32) + part(0)
    patch_grad = call(
        final_kernel,
        sds((tok, model), BF16),
        ids,
        total[:tok],
        swap(total[tok:].astype(BF16)),
        x_own,
    )
    return (prediction[None], patch_grad[None])


def solution(mesh):
    group = ("section", "mp")
    in_specs = (
        P("dp", group, None),
        P("dp", group),
        P("section", None, "mp"),
        P("mp", "section"),
        P(group, None),
        P(),
        P(group, None),
        P(),
        P(),
        P(),
        P("dp", group, None),
    )
    out_specs = (P("dp", group, None), P("dp", group, None))
    return jax.shard_map(shards, mesh=mesh, in_specs=in_specs, out_specs=out_specs, check_vma=False)
```

profile of v0, /device:TPU:1, one launch (start us, length us, event | category | flops | bytes accessed | tf_op | source)
XLA Modules:
  0.0 243.8 jit_solution(17003160834357484435)
XLA Ops:
  8.2 3.3 %collective-permute-start = (bf16[16,3072]{1,0:T(8,128)(2,1)S(1)}, bf16[16,3072]{1,0:T(8,128)(2,1)S(1)}, u32[]{:S(2)}, u32[]{:S(2)}) collective-permute-start(bf16[16,3072]{1,0:T(8,128)(2,1)S(1)} %get-tuple-element.69), channel_id=1, source_target_pairs={{0,128},{128,0},{1,129},{129,1},{2,130},{130,2},{3,131},{131,3},{4... | collective-permute-start | bytes 294920 | tf_op jit(solution)/shard_map/ppermute | solution.py:422
  12.7 28.0 %all-gather = bf16[1024,384]{0,1:T(8,128)(2,1)} all-gather(bf16[128,384]{0,1:T(8,128)(2,1)S(1)} %dynamic-slice_bitcast_fusion), channel_id=2, replica_groups=mesh['section'=2,'mp'=8,'dp'=16] {'mp'}, dimensions={0}, use_global_device_ids=true | all-gather | bytes 884736 | tf_op jit(solution)/shard_map/all_gather | solution.py:433
  44.8 3.3 %collective-permute-done.2.refs_2_ = bf16[32,3072]{1,0:T(8,128)(2,1)S(1)} collective-permute-done((bf16[32,3072]{1,0:T(8,128)(2,1)}, bf16[32,3072]{1,0:T(8,128)(2,1)S(1)}, u32[]{:S(2)}, u32[]{:S(2)}) %collective-permute-start.2) | collective-permute-done | bytes 196640 | tf_op jit(solution)/shard_map/ppermute | solution.py:425
  49.8 4.4 %collective-permute-done.4.refs_4_ = bf16[32,3072]{1,0:T(8,128)(2,1)S(1)} collective-permute-done((bf16[32,3072]{1,0:T(8,128)(2,1)S(1)}, bf16[32,3072]{1,0:T(8,128)(2,1)S(1)}, u32[]{:S(2)}, u32[]{:S(2)}) %collective-permute-start.4) | collective-permute-done | bytes 196640 | tf_op jit(solution)/shard_map/ppermute | solution.py:425
  58.3 10.4 %collective-permute-start.10 = (bf16[128,384]{1,0:T(8,128)(2,1)S(1)}, bf16[128,384]{1,0:T(8,128)(2,1)S(1)}, u32[]{:S(2)}, u32[]{:S(2)}) collective-permute-start(bf16[128,384]{1,0:T(8,128)(2,1)S(1)} %get-tuple-element.38), channel_id=1, source_target_pairs={{0,128},{128,0},{1,129},{129,1},{2,130},{130,2},{3,131},{131,3},{4... | collective-permute-start | bytes 294920 | tf_op jit(solution)/shard_map/ppermute | solution.py:422
  68.7 3.0 %copy-done = bf16[3072,3,384]{2,0,1:T(8,128)(2,1)S(1)} copy-done((bf16[3072,3,384]{2,0,1:T(8,128)(2,1)S(1)}, bf16[3072,3,384]{2,0,1:T(8,128)(2,1)}, u32[]{:S(2)}) %copy-start) | copy-done | bytes 7077912
  71.7 6.4 %shard_map.122 = (bf16[2,8,16,3072]{3,2,1,0:T(8,128)(2,1)S(1)}, f32[272,1152]{1,0:T(8,128)S(1)}, bf16[272,1152]{1,0:T(8,128)(2,1)}, f32[256,128]{1,0:T(8,128)S(1...) custom-call(s32[3]{0:T(128)S(1)} %pad_add_fusion.ids, bf16[32,3072]{1,0:T(8,128)(2,1)S(1)} %copy-done.11, ...), custom_call_target="tpu_custom_call" | custom-call | tf_op jit(solution)/shard_map/pallas_call | solution.py:57
  78.8 6.5 %collective-permute-start.8 = (bf16[272,1152]{1,0:T(8,128)(2,1)}, bf16[272,1152]{1,0:T(8,128)(2,1)}, u32[]{:S(2)}, u32[]{:S(2)}) collective-permute-start(bf16[272,1152]{1,0:T(8,128)(2,1)} %get-tuple-element.34), channel_id=1, source_target_pairs={{0,128},{128,0},{1,129},{129,1},{2,130},{130,2},{3,131},{131,3},{4... | collective-permute-start | bytes 1880072 | tf_op jit(solution)/shard_map/ppermute | solution.py:422
  86.2 4.0 %all-to-all-start = ((bf16[4,128,384]{2,1,0:T(8,128)(2,1)}), bf16[4,128,384]{2,1,0:T(8,128)(2,1)S(1)}, u32[]{:S(2)}, u32[]{:S(2)}) async-start(bf16[4,128,384]{2,1,0:T(8,128)(2,1)} %broadcast_in_dim.19), calls=%async_computation | async-start | bytes 786432 | tf_op jit(solution)/shard_map/all_to_all | solution.py:481
  102.6 12.9 %all_to_all.25 = bf16[8,16,512]{2,1,0:T(8,128)(2,1)} all-to-all(bf16[8,16,512]{2,1,0:T(8,128)(2,1)} %bitcast.58), channel_id=1, replica_groups=mesh['section'=2,'mp'=8,'dp'=16] {'mp'}, dimensions={0} | all-to-all | bytes 262144 | tf_op jit(solution)/shard_map/all_to_all | solution.py:428
  117.9 10.4 %all_to_all.26 = bf16[8,16,512]{2,1,0:T(8,128)(2,1)S(1)} all-to-all(bf16[8,16,512]{2,1,0:T(8,128)(2,1)S(1)} %broadcast_in_dim.20), channel_id=1, replica_groups=mesh['section'=2,'mp'=8,'dp'=16] {'mp'}, dimensions={0} | all-to-all | bytes 262144 | tf_op jit(solution)/shard_map/all_to_all | solution.py:428
  128.3 3.2 %collective-permute-start.12 = (bf16[128,512]{1,0:T(8,128)(2,1)S(1)}, bf16[128,512]{1,0:T(8,128)(2,1)S(1)}, u32[]{:S(2)}, u32[]{:S(2)}) collective-permute-start(bf16[128,512]{1,0:T(8,128)(2,1)S(1)} %bitcast.55), channel_id=1, source_target_pairs={{0,128},{128,0},{1,129},{129,1},{2,130},{130,2},{3,131},{131,3},{4... | collective-permute-start | bytes 393224 | tf_op jit(solution)/shard_map/ppermute | solution.py:422
  135.6 7.7 %shard_map.126 = (bf16[64,768]{1,0:T(8,128)(2,1)}, f32[128,512]{1,0:T(8,128)S(1)}, bf16[128,512]{1,0:T(8,128)(2,1)S(1)}) custom-call(s32[3]{0:T(128)S(1)} %pad_add_fusion.ids, s32[1,256]{1,0:T(1,128)S(1)} %get-tuple-element.42.vis_row, bf16[128,512]{1,0:T(8,128)(2,1)S(1)} %bitcast.56, bf16[128,512]{1,0:T(8,128)(2,1)S(1)} %collective-permute-done.12.emb_other, ...), custom_call_target="tpu_custom_call" | custom-call | tf_op jit(solution)/shard_map/pallas_call | solution.py:57
  143.3 10.2 %collective-permute-start.13 = (bf16[128,512]{1,0:T(8,128)(2,1)S(1)}, bf16[128,512]{1,0:T(8,128)(2,1)S(1)}, u32[]{:S(2)}, u32[]{:S(2)}) collective-permute-start(bf16[128,512]{1,0:T(8,128)(2,1)S(1)} %get-tuple-element.52), channel_id=1, source_target_pairs={{0,128},{128,0},{1,129},{129,1},{2,130},{130,2},{3,131},{131,3},{4... | collective-permute-start | bytes 393224 | tf_op jit(solution)/shard_map/ppermute | solution.py:422
  154.9 11.0 %all_to_all.27 = bf16[8,16,512]{2,1,0:T(8,128)(2,1)S(1)} all-to-all(bf16[8,16,512]{2,1,0:T(8,128)(2,1)S(1)} %bitcast.59), channel_id=1, replica_groups=mesh['section'=2,'mp'=8,'dp'=16] {'mp'}, dimensions={0} | all-to-all | bytes 262144 | tf_op jit(solution)/shard_map/all_to_all | solution.py:428
  165.9 10.4 %all_to_all.28 = bf16[8,16,512]{2,1,0:T(8,128)(2,1)S(1)} all-to-all(bf16[8,16,512]{2,1,0:T(8,128)(2,1)S(1)} %broadcast_in_dim.22), channel_id=1, replica_groups=mesh['section'=2,'mp'=8,'dp'=16] {'mp'}, dimensions={0} | all-to-all | bytes 262144 | tf_op jit(solution)/shard_map/all_to_all | solution.py:428
  179.8 3.0 %copy-done.1 = bf16[3072,3,384]{2,0,1:T(8,128)(2,1)S(1)} copy-done((bf16[3072,3,384]{2,0,1:T(8,128)(2,1)S(1)}, bf16[3072,3,384]{2,0,1:T(8,128)(2,1)}, u32[]{:S(2)}) %copy-start.1) | copy-done | bytes 7077912
  188.6 5.4 %shard_map.127 = (bf16[64,3200]{1,0:T(8,128)(2,1)S(1)}, bf16[256,1152]{1,0:T(8,128)(2,1)S(1)}, f32[256,384]{1,0:T(8,128)S(1)}) custom-call(s32[3]{0:T(128)S(1)} %pad_add_fusion.ids, bf16[128,512]{1,0:T(8,128)(2,1)S(1)} %bitcast.54, bf16[128,512]{1,0:T(8,128)(2,1)S(1)} %collective-permute-done.14.g_other, bf16[512,384]{1,0:T(8,128)(2,1)S(1)} %bitcast.49, ...), custom_call_target="tpu_custom_call" | custom-call | tf_op jit(solution)/shard_map/pallas_call | solution.py:57
  198.4 3.0 %copy-done.2 = bf16[3072,3,384]{2,0,1:T(8,128)(2,1)S(1)} copy-done((bf16[3072,3,384]{2,0,1:T(8,128)(2,1)S(1)}, bf16[3072,3,384]{2,0,1:T(8,128)(2,1)}, u32[]{:S(2)}) %copy-start.2) | copy-done | bytes 7077912
  204.4 4.7 %shard_map.128 = bf16[8,32,3200]{2,1,0:T(8,128)(2,1)S(1)} custom-call(s32[3]{0:T(128)S(1)} %pad_add_fusion.ids, bf16[256,1152]{1,0:T(8,128)(2,1)S(1)} %copy-done.13, f32[256,384]{1,0:T(8,128)S(1)} %copy-done.25, f32[256,128]{1,0:T(8,128)S(1)} %copy-done.16, bf16[2,8,16,3072]{3,2,1,0:T(8,128)(2,1)S(1)} %get-tuple-element.58.x_in, ...), custom_call_target="tpu_custom_call" | custom-call | tf_op jit(solution)/shard_map/pallas_call | solution.py:57
  210.2 6.8 %collective-permute-done.16 = bf16[32,3200]{1,0:T(8,128)(2,1)S(1)} collective-permute-done((bf16[32,3200]{1,0:T(8,128)(2,1)S(1)}, bf16[32,3200]{1,0:T(8,128)(2,1)S(1)}, u32[]{:S(2)}, u32[]{:S(2)}) %collective-permute-start.16) | collective-permute-done | bytes 204832 | tf_op jit(solution)/shard_map/ppermute | solution.py:425
  220.8 3.1 %collective-permute-done.17 = bf16[32,3200]{1,0:T(8,128)(2,1)S(1)} collective-permute-done((bf16[32,3200]{1,0:T(8,128)(2,1)S(1)}, bf16[32,3200]{1,0:T(8,128)(2,1)S(1)}, u32[]{:S(2)}, u32[]{:S(2)}) %collective-permute-start.17) | collective-permute-done | bytes 204832 | tf_op jit(solution)/shard_map/ppermute | solution.py:425
  226.9 3.1 %collective-permute-done.18 = bf16[32,3200]{1,0:T(8,128)(2,1)S(1)} collective-permute-done((bf16[32,3200]{1,0:T(8,128)(2,1)S(1)}, bf16[32,3200]{1,0:T(8,128)(2,1)S(1)}, u32[]{:S(2)}, u32[]{:S(2)}) %collective-permute-start.18) | collective-permute-done | bytes 204832 | tf_op jit(solution)/shard_map/ppermute | solution.py:425
  230.0 4.2 %collective-permute-start.22 = (bf16[16,3200]{1,0:T(8,128)(2,1)S(1)}, bf16[16,3200]{1,0:T(8,128)(2,1)S(1)}, u32[]{:S(2)}, u32[]{:S(2)}) collective-permute-start(bf16[16,3200]{1,0:T(8,128)(2,1)S(1)} %slice.20), channel_id=1, source_target_pairs={{0,128},{128,0},{1,129},{129,1},{2,130},{130,2},{3,131},{131,3},{4... | collective-permute-start | bytes 307208 | tf_op jit(solution)/shard_map/ppermute | solution.py:422
  (145 shorter events, 60.7 us)
Async XLA Ops:
  7.2 95.5 %all-gather.4.cloned.1.call-start = ((), (), s32[]{:S(2)}) async-start(), calls=%async_computation.5 | async-start | bytes 1392640 | tf_op jit(solution)/shard_map/all_gather | solution.py:454
  8.2 4.4 %collective-permute-start = (bf16[16,3072]{1,0:T(8,128)(2,1)S(1)}, bf16[16,3072]{1,0:T(8,128)(2,1)S(1)}, u32[]{:S(2)}, u32[]{:S(2)}) collective-permute-start(bf16[16,3072]{1,0:T(8,128)(2,1)S(1)} %get-tuple-element.69), channel_id=1, source_target_pairs={{0,128},{128,0},{1,129},{129,1},{2,130},{130,2},{3,131},{131,3},{4... | collective-permute-start | bytes 294920 | tf_op jit(solution)/shard_map/ppermute | solution.py:422
  12.6 29.6 %collective-permute-start.1 = (bf16[32,3072]{1,0:T(8,128)(2,1)S(1)}, bf16[32,3072]{1,0:T(8,128)(2,1)}, u32[]{:S(2)}, u32[]{:S(2)}) collective-permute-start(bf16[32,3072]{1,0:T(8,128)(2,1)S(1)} %pad_maximum_fusion.refs_0_), channel_id=1, source_target_pairs={{0,16},{16,32},{32,48},{48,64},{64,80},{80,96},{96,112},{112,0},{1... | collective-permute-start | bytes 589832 | tf_op jit(solution)/shard_map/ppermute | solution.py:425
  43.2 4.8 %collective-permute-start.2 = (bf16[32,3072]{1,0:T(8,128)(2,1)}, bf16[32,3072]{1,0:T(8,128)(2,1)S(1)}, u32[]{:S(2)}, u32[]{:S(2)}) collective-permute-start(bf16[32,3072]{1,0:T(8,128)(2,1)} %copy-done.10), channel_id=1, source_target_pairs={{0,112},{16,0},{32,16},{48,32},{64,48},{80,64},{96,80},{112,96},{1... | collective-permute-start | bytes 589832 | tf_op jit(solution)/shard_map/ppermute | solution.py:425
  43.8 5.9 %collective-permute-start.3 = (bf16[32,3072]{1,0:T(8,128)(2,1)}, bf16[32,3072]{1,0:T(8,128)(2,1)S(1)}, u32[]{:S(2)}, u32[]{:S(2)}) collective-permute-start(bf16[32,3072]{1,0:T(8,128)(2,1)} %collective-permute-done.1.refs_1_), channel_id=1, source_target_pairs={{0,16},{16,32},{32,48},{48,64},{64,80},{80,96},{96,112},{112,0},{1... | collective-permute-start | bytes 589832 | tf_op jit(solution)/shard_map/ppermute | solution.py:425
  48.0 6.1 %collective-permute-start.4 = (bf16[32,3072]{1,0:T(8,128)(2,1)S(1)}, bf16[32,3072]{1,0:T(8,128)(2,1)S(1)}, u32[]{:S(2)}, u32[]{:S(2)}) collective-permute-start(bf16[32,3072]{1,0:T(8,128)(2,1)S(1)} %collective-permute-done.2.refs_2_), channel_id=1, source_target_pairs={{0,112},{16,0},{32,16},{48,32},{64,48},{80,64},{96,80},{112,96},{1... | collective-permute-start | bytes 589832 | tf_op jit(solution)/shard_map/ppermute | solution.py:425
  49.8 7.0 %collective-permute-start.5 = (bf16[32,3072]{1,0:T(8,128)(2,1)S(1)}, bf16[32,3072]{1,0:T(8,128)(2,1)S(1)}, u32[]{:S(2)}, u32[]{:S(2)}) collective-permute-start(bf16[32,3072]{1,0:T(8,128)(2,1)S(1)} %collective-permute-done.3.refs_3_), channel_id=1, source_target_pairs={{0,16},{16,32},{32,48},{48,64},{64,80},{80,96},{96,112},{112,0},{1... | collective-permute-start | bytes 589832 | tf_op jit(solution)/shard_map/ppermute | solution.py:425
  54.2 14.5 %collective-permute-start.6 = (bf16[32,3072]{1,0:T(8,128)(2,1)S(1)}, bf16[32,3072]{1,0:T(8,128)(2,1)S(1)}, u32[]{:S(2)}, u32[]{:S(2)}) collective-permute-start(bf16[32,3072]{1,0:T(8,128)(2,1)S(1)} %collective-permute-done.4.refs_4_), channel_id=1, source_target_pairs={{0,112},{16,0},{32,16},{48,32},{64,48},{80,64},{96,80},{112,96},{1... | collective-permute-start | bytes 589832 | tf_op jit(solution)/shard_map/ppermute | solution.py:425
  56.8 11.9 %collective-permute-start.7 = (bf16[32,3072]{1,0:T(8,128)(2,1)S(1)}, bf16[32,3072]{1,0:T(8,128)(2,1)S(1)}, u32[]{:S(2)}, u32[]{:S(2)}) collective-permute-start(bf16[32,3072]{1,0:T(8,128)(2,1)S(1)} %collective-permute-done.5.refs_5_), channel_id=1, source_target_pairs={{0,16},{16,32},{32,48},{48,64},{64,80},{80,96},{96,112},{112,0},{1... | collective-permute-start | bytes 589832 | tf_op jit(solution)/shard_map/ppermute | solution.py:425
  58.3 27.0 %collective-permute-start.10 = (bf16[128,384]{1,0:T(8,128)(2,1)S(1)}, bf16[128,384]{1,0:T(8,128)(2,1)S(1)}, u32[]{:S(2)}, u32[]{:S(2)}) collective-permute-start(bf16[128,384]{1,0:T(8,128)(2,1)S(1)} %get-tuple-element.38), channel_id=1, source_target_pairs={{0,128},{128,0},{1,129},{129,1},{2,130},{130,2},{3,131},{131,3},{4... | collective-permute-start | bytes 294920 | tf_op jit(solution)/shard_map/ppermute | solution.py:422
  78.8 13.4 %collective-permute-start.8 = (bf16[272,1152]{1,0:T(8,128)(2,1)}, bf16[272,1152]{1,0:T(8,128)(2,1)}, u32[]{:S(2)}, u32[]{:S(2)}) collective-permute-start(bf16[272,1152]{1,0:T(8,128)(2,1)} %get-tuple-element.34), channel_id=1, source_target_pairs={{0,128},{128,0},{1,129},{129,1},{2,130},{130,2},{3,131},{131,3},{4... | collective-permute-start | bytes 1880072 | tf_op jit(solution)/shard_map/ppermute | solution.py:422
  86.2 13.4 %all-to-all-start = ((bf16[4,128,384]{2,1,0:T(8,128)(2,1)}), bf16[4,128,384]{2,1,0:T(8,128)(2,1)S(1)}, u32[]{:S(2)}, u32[]{:S(2)}) async-start(bf16[4,128,384]{2,1,0:T(8,128)(2,1)} %broadcast_in_dim.19), calls=%async_computation | async-start | bytes 786432 | tf_op jit(solution)/shard_map/all_to_all | solution.py:481
  90.8 10.1 %collective-permute-start.11 = (bf16[128,512]{1,0:T(8,128)(2,1)}, bf16[128,512]{1,0:T(8,128)(2,1)}, u32[]{:S(2)}, u32[]{:S(2)}) collective-permute-start(bf16[128,512]{1,0:T(8,128)(2,1)} %copy-done.35), channel_id=1, source_target_pairs={{0,128},{128,0},{1,129},{129,1},{2,130},{130,2},{3,131},{131,3},{4... | collective-permute-start | bytes 393224 | tf_op jit(solution)/shard_map/ppermute | solution.py:422
  128.3 7.3 %collective-permute-start.12 = (bf16[128,512]{1,0:T(8,128)(2,1)S(1)}, bf16[128,512]{1,0:T(8,128)(2,1)S(1)}, u32[]{:S(2)}, u32[]{:S(2)}) collective-permute-start(bf16[128,512]{1,0:T(8,128)(2,1)S(1)} %bitcast.55), channel_id=1, source_target_pairs={{0,128},{128,0},{1,129},{129,1},{2,130},{130,2},{3,131},{131,3},{4... | collective-permute-start | bytes 393224 | tf_op jit(solution)/shard_map/ppermute | solution.py:422
  143.3 11.5 %collective-permute-start.13 = (bf16[128,512]{1,0:T(8,128)(2,1)S(1)}, bf16[128,512]{1,0:T(8,128)(2,1)S(1)}, u32[]{:S(2)}, u32[]{:S(2)}) collective-permute-start(bf16[128,512]{1,0:T(8,128)(2,1)S(1)} %get-tuple-element.52), channel_id=1, source_target_pairs={{0,128},{128,0},{1,129},{129,1},{2,130},{130,2},{3,131},{131,3},{4... | collective-permute-start | bytes 393224 | tf_op jit(solution)/shard_map/ppermute | solution.py:422
  176.3 3.4 %collective-permute-start.14 = (bf16[128,512]{1,0:T(8,128)(2,1)S(1)}, bf16[128,512]{1,0:T(8,128)(2,1)S(1)}, u32[]{:S(2)}, u32[]{:S(2)}) collective-permute-start(bf16[128,512]{1,0:T(8,128)(2,1)S(1)} %bitcast.53), channel_id=1, source_target_pairs={{0,128},{128,0},{1,129},{129,1},{2,130},{130,2},{3,131},{131,3},{4... | collective-permute-start | bytes 393224 | tf_op jit(solution)/shard_map/ppermute | solution.py:422
  195.7 13.3 %collective-permute-start.15 = (bf16[32,3200]{1,0:T(8,128)(2,1)}, bf16[32,3200]{1,0:T(8,128)(2,1)}, u32[]{:S(2)}, u32[]{:S(2)}) collective-permute-start(bf16[32,3200]{1,0:T(8,128)(2,1)} %get-tuple-element.66), channel_id=1, source_target_pairs={{0,16},{16,32},{32,48},{48,64},{64,80},{80,96},{96,112},{112,0},{1... | collective-permute-start | bytes 614408 | tf_op jit(solution)/shard_map/ppermute | solution.py:425
  196.0 14.2 %collective-permute-start.19 = (bf16[32,3200]{1,0:T(8,128)(2,1)S(1)}, bf16[32,3200]{1,0:T(8,128)(2,1)}, u32[]{:S(2)}, u32[]{:S(2)}) collective-permute-start(bf16[32,3200]{1,0:T(8,128)(2,1)S(1)} %get-tuple-element.67), channel_id=1, source_target_pairs={{0,112},{16,0},{32,16},{48,32},{64,48},{80,64},{96,80},{112,96},{1... | collective-permute-start | bytes 614408 | tf_op jit(solution)/shard_map/ppermute | solution.py:425
  210.0 7.0 %collective-permute-start.16 = (bf16[32,3200]{1,0:T(8,128)(2,1)S(1)}, bf16[32,3200]{1,0:T(8,128)(2,1)S(1)}, u32[]{:S(2)}, u32[]{:S(2)}) collective-permute-start(bf16[32,3200]{1,0:T(8,128)(2,1)S(1)} %fusion.4), channel_id=1, source_target_pairs={{0,16},{16,32},{32,48},{48,64},{64,80},{80,96},{96,112},{112,0},{1... | collective-permute-start | bytes 614408 | tf_op jit(solution)/shard_map/ppermute | solution.py:425
  218.0 5.9 %collective-permute-start.17 = (bf16[32,3200]{1,0:T(8,128)(2,1)S(1)}, bf16[32,3200]{1,0:T(8,128)(2,1)S(1)}, u32[]{:S(2)}, u32[]{:S(2)}) collective-permute-start(bf16[32,3200]{1,0:T(8,128)(2,1)S(1)} %get-tuple-element.64), channel_id=1, source_target_pairs={{0,16},{16,32},{32,48},{48,64},{64,80},{80,96},{96,112},{112,0},{1... | collective-permute-start | bytes 614408 | tf_op jit(solution)/shard_map/ppermute | solution.py:425
  218.1 5.8 %collective-permute-start.20 = (bf16[32,3200]{1,0:T(8,128)(2,1)S(1)}, bf16[32,3200]{1,0:T(8,128)(2,1)S(1)}, u32[]{:S(2)}, u32[]{:S(2)}) collective-permute-start(bf16[32,3200]{1,0:T(8,128)(2,1)S(1)} %get-tuple-element.65), channel_id=1, source_target_pairs={{0,112},{16,0},{32,16},{48,32},{64,48},{80,64},{96,80},{112,96},{1... | collective-permute-start | bytes 614408 | tf_op jit(solution)/shard_map/ppermute | solution.py:425
  224.0 5.9 %collective-permute-start.18 = (bf16[32,3200]{1,0:T(8,128)(2,1)S(1)}, bf16[32,3200]{1,0:T(8,128)(2,1)S(1)}, u32[]{:S(2)}, u32[]{:S(2)}) collective-permute-start(bf16[32,3200]{1,0:T(8,128)(2,1)S(1)} %get-tuple-element.62), channel_id=1, source_target_pairs={{0,16},{16,32},{32,48},{48,64},{64,80},{80,96},{96,112},{112,0},{1... | collective-permute-start | bytes 614408 | tf_op jit(solution)/shard_map/ppermute | solution.py:425
  224.1 5.8 %collective-permute-start.21 = (bf16[32,3200]{1,0:T(8,128)(2,1)S(1)}, bf16[32,3200]{1,0:T(8,128)(2,1)S(1)}, u32[]{:S(2)}, u32[]{:S(2)}) collective-permute-start(bf16[32,3200]{1,0:T(8,128)(2,1)S(1)} %get-tuple-element.63), channel_id=1, source_target_pairs={{0,112},{16,0},{32,16},{48,32},{64,48},{80,64},{96,80},{112,96},{1... | collective-permute-start | bytes 614408 | tf_op jit(solution)/shard_map/ppermute | solution.py:425
  230.0 5.2 %collective-permute-start.22 = (bf16[16,3200]{1,0:T(8,128)(2,1)S(1)}, bf16[16,3200]{1,0:T(8,128)(2,1)S(1)}, u32[]{:S(2)}, u32[]{:S(2)}) collective-permute-start(bf16[16,3200]{1,0:T(8,128)(2,1)S(1)} %slice.20), channel_id=1, source_target_pairs={{0,128},{128,0},{1,129},{129,1},{2,130},{130,2},{3,131},{131,3},{4... | collective-permute-start | bytes 307208 | tf_op jit(solution)/shard_map/ppermute | solution.py:422
  (39 other events, 366.7 us)
Sparse Core Ops, SparseCore 0:
  43.3 42.4 all-gather.3
where the time goes:
time: 248 us; the launch traced here: 244 us
  blocking collectives  72.8 us (29%)
  starting transfers between devices  58.9 us (24%)
  Pallas kernels  32.3 us (13%)
  local copies, waits for them, and re-layouts  32 us (13%)
  waiting for transfers between devices  25.7 us (10%)
  between operations  14.7 us (6%)
  other arithmetic  6.28 us (3%)
    all_to_all x4, blocking collectives, exchange(): return lax.all_to_all(value, axis, 0, 0, tiled=True)  44.8 us
    ppermute x9, starting transfers between devices, swap(): return lax.ppermute(value, 'section', [(0, 1), (1, 0)])  40.9 us
    pallas_call x8, Pallas kernels, call(): pl.pallas_call(kernel, out_shape=out_shape, in_specs=specs, out_specs=jax...  32.3 us
    all_gather x1, blocking collectives, shards(): lax.all_gather(lax.dynamic_slice_in_dim(embed_weight, place * dec_cols, d...  28 us
    unnamed x76, local copies, waits for them, and re-layouts  25.8 us
    ppermute x14, waiting for transfers between devices, shift(): return lax.ppermute(value, 'mp', [(i, (i + by) % 8) for i in range(8)])  21 us
    ppermute x14, starting transfers between devices, shift(): return lax.ppermute(value, 'mp', [(i, (i + by) % 8) for i in range(8)])  14 us
  transfers between devices with their start and end apart: 25, of which 10 were waited for; matrix products, arithmetic and copies ran while one was open for 3% of the time, Pallas kernels for 7%

commit v1 on v0

--- a/solution.py
+++ b/solution.py
@@ -50,99 +50,133 @@
     return out
 
 
-def call(kernel, out_shape, *args, scratch=(), far=(), limit=24):
+def call(kernel, outs, *args, scratch=(), far=(), far_out=(), copies=0, limit=24):
     specs = [pl.BlockSpec(memory_space=pltpu.SMEM)]
     for at in range(1, len(args)):
-        specs.append(pl.BlockSpec(memory_space=pl.ANY if at in far else pltpu.VMEM))
+        specs.append(pl.BlockSpec(memory_space=pltpu.HBM if at in far else pltpu.VMEM))
+    out_specs = [
+        pl.BlockSpec(memory_space=pltpu.HBM if at in far_out else pltpu.VMEM) for at in range(len(outs))
+    ]
+    scratch = [pltpu.VMEM(shape.shape, shape.dtype) for shape in scratch]
+    if copies:
+        scratch.append(pltpu.SemaphoreType.DMA((copies,)))
     return pl.pallas_call(
         kernel,
-        out_shape=out_shape,
+        out_shape=tuple(outs),
         in_specs=specs,
-        out_specs=jax.tree.map(lambda _: pl.BlockSpec(memory_space=pltpu.VMEM), out_shape),
-        scratch_shapes=list(scratch),
+        out_specs=tuple(out_specs),
+        scratch_shapes=scratch,
         compiler_params=pltpu.CompilerParams(vmem_limit_bytes=limit * 2**20),
     )(*args)
 
 
-def sds(shape, dtype):
-    return jax.ShapeDtypeStruct(shape, dtype)
-
-
-def fetch(w, held, sems):
-    copies = [pltpu.make_async_copy(w.at[at], held.at[at], sems.at[at]) for at in range(3)]
+def start(sems, first, *pairs):
+    copies = [
+        pltpu.make_async_copy(source, target, sems.at[first + at]) for at, (source, target) in enumerate(pairs)
+    ]
     for copy in copies:
         copy.start()
     return copies
 
 
-def fold_kernel(ids, pieces, wo, out, out_low):
-    slab = wo.shape[1] // 8
-    total = dot_nt(pieces[0], wo[:, :slab])
-    for at in range(1, 8):
-        total = total + dot_nt(pieces[at], wo[:, at * slab : (at + 1) * slab])
-    out[...] = total
-    out_low[...] = total.astype(BF16)
+def finish(copies):
+    for copy in copies:
+        copy.wait()
+
+
+def sds(shape, dtype):
+    return jax.ShapeDtypeStruct(shape, dtype)
+
+
+def fold_kernel(ids, *refs):
+    chunks, wo, out, wt = refs[:8], refs[8], refs[9], refs[10]
+    half = wo.shape[1]
+    slab = half // 8
+    for chunk, offset in zip(chunks, OFFSETS):
+        column = pl.multiple_of(lax.rem(ids[1] + offset + 8, 8) * slab, 128)
+        for piece in range(wt.shape[0] // 32):
+            wt[piece * 32 : piece * 32 + 32, pl.ds(column, slab)] = chunk[
+                :, half + piece * slab : half + (piece + 1) * slab
+            ]
+    total = dot_nt(wt[...], wo[...]).astype(BF16)
+    for at in range(out.shape[0]):
+        out[at] = total
+
+
+def split3(values):
+    first = values.astype(BF16).astype(F32)
+    second = (values - first).astype(BF16).astype(F32)
+    return [first, second, values - first - second]
 
 
 def project_kernel(ids, *refs):
     chunks = refs[:8]
     w, we = refs[8:10]
-    x_out, p_own, p_send, stats, xp_own, xp_send = refs[10:16]
-    xc, held, sems = refs[16:]
-    copies = fetch(w, held, sems)
-    half = held.shape[1]
-    width = held.shape[2]
+    x_out, p_own, p_send, xp_own, xp_send = refs[10:15]
+    xs, xc, held, xp, sems = refs[15:]
+    loads = start(sems, 0, *[(w.at[at], held.at[at]) for at in range(3)])
+    half, width = held.shape[1:]
     slab = half // 8
-    tok = x_out.shape[2]
+    tok = xs.shape[2]
     group = 8 * tok
     m = ids[1]
     for chunk, offset in zip(chunks, OFFSETS):
         at = lax.rem(m + offset + 8, 8)
-        value = chunk[...]
-        x_out[0, at] = value[:tok]
-        x_out[1, at] = value[tok:]
+        value = chunk[:, :half]
+        xs[0, at] = value[:tok]
+        xs[1, at] = value[tok:]
         wide = value.astype(F32)
         centre = jnp.mean(wide, axis=1, keepdims=True)
         centered = wide - centre
         spread = jnp.sum(centered * centered, axis=1, keepdims=True)
         low = centered.astype(BF16)
-        both = lanes((centre, spread), 2 * tok)
+        own = lanes((centre, spread), 2 * tok)
+        send = lanes(split3(centre) + split3(spread), 2 * tok).astype(BF16)
         row = pl.multiple_of(at * tok, tok)
-        xc[pl.ds(row, tok), :] = low[:tok]
-        xc[pl.ds(row + group, tok), :] = low[tok:]
-        stats[pl.ds(row, tok), :] = both[:tok]
-        stats[pl.ds(row + group, tok), :] = both[tok:]
+        for rel in range(2):
+            part = slice(rel * tok, (rel + 1) * tok)
+            xc[pl.ds(row + rel * group, tok), :] = low[part]
+            p_own[pl.ds(row + rel * group, tok), 3 * width :] = own[part]
+            p_send[pl.ds(row + rel * group, tok), 3 * width :] = send[part]
+    stores = start(sems, 3, (xs, x_out))
     xc[2 * group :, :] = jnp.ones((16, half), BF16)
+    p_own[2 * group :, 3 * width :] = jnp.zeros((16, 128), F32)
+    p_send[2 * group :, 3 * width :] = jnp.zeros((16, 128), BF16)
     for at in range(3):
-        copies[at].wait()
+        loads[at].wait()
         product = dot(xc[...], held[at])
         p_own[:, at * width : (at + 1) * width] = product
         p_send[:, at * width : (at + 1) * width] = product.astype(BF16)
     column = pl.multiple_of(m * slab, 128)
-    raw = jnp.concatenate(
-        [x_out[0, :, :, pl.ds(column, slab)], x_out[1, :, :, pl.ds(column, slab)]]
-    ).reshape(2 * group, slab)
-    part = dot(raw, we[...])
-    xp_own[...] = part[:group]
+    raw = jnp.concatenate([xs[0, :, :, pl.ds(column, slab)], xs[1, :, :, pl.ds(column, slab)]])
+    part = dot(raw.reshape(2 * group, slab), we[...])
+    xp[...] = part[:group]
+    stores += start(sems, 4, (xp, xp_own))
     xp_send[...] = part[group:].astype(BF16)
-
-
-def attend_kernel(ids, p_own, p_other, st_own, st_other, att, e_out, q_out, k_out, v_out, aux):
-    rows = st_own.shape[0]
+    finish(stores)
+
+
+def attend_kernel(ids, p_own, p_other, att, *refs):
+    saved = refs[:5]
+    e_out, q_out, k_out, v_out, aux = refs[5:10]
+    sems = refs[10]
+    rows = p_own.shape[0] - 16
     group = rows // 2
-    width = p_own.shape[1] // 3
+    width = (p_own.shape[1] - 128) // 3
     heads = width // HD
     model = 2 * 8 * width
-    stats_other = jnp.concatenate([st_other[group:, :], st_other[:group, :]])
-    m_own, s_own = st_own[:, 0:1], st_own[:, 1:2]
-    m_other, s_other = stats_other[:, 0:1], stats_other[:, 1:2]
+    stats = p_other[:rows, 3 * width :].astype(F32)
+    stats = jnp.concatenate([stats[group:, :], stats[:group, :]])
+    m_own, s_own = p_own[:rows, 3 * width : 3 * width + 1], p_own[:rows, 3 * width + 1 : 3 * width + 2]
+    m_other = stats[:, 0:1] + stats[:, 1:2] + stats[:, 2:3]
+    s_other = stats[:, 3:4] + stats[:, 4:5] + stats[:, 5:6]
     gap = (m_own - m_other) * 0.5
     centre = (m_own + m_other) * 0.5
     inverse = lax.rsqrt((s_own + s_other) / model + gap * gap + EPSILON)
-    slope = p_own[rows : rows + 1, :] - p_other[rows : rows + 1, :].astype(F32)
-    columns = [centre, inverse]
+    slope = p_own[rows : rows + 1, : 3 * width] - p_other[rows : rows + 1, : 3 * width].astype(F32)
     inv_q, inv_k, inv_l = [], [], []
     factor = LOG2E * HD**-0.5
+    stores = []
 
     def mixture(at):
         cols = slice(at * HD, (at + 1) * HD)
@@ -157,15 +191,35 @@
         e = jnp.exp2(dot_nt(q_hat.astype(BF16), k_hat.astype(BF16)) * factor)
         l_inv = 1.0 / jnp.sum(e, axis=1, keepdims=True)
         e_low = e.astype(BF16)
+        e_out[head] = e_low
+        stores += start(sems, head, (e_out.at[head], saved[0].at[head]))
         att[:, cols] = (dot(e_low[:group], v_low) * l_inv[:group]).astype(BF16)
-        e_out[head] = e_low
         q_out[:, cols] = q_hat
         k_out[:, cols] = k_hat
         v_out[:, cols] = v_low
         inv_q.append(q_inv)
         inv_k.append(k_inv)
         inv_l.append(l_inv)
-    aux[...] = lanes(columns + inv_l + inv_q + inv_k, rows)
+    aux[...] = lanes([centre, inverse] + inv_l + inv_q + inv_k, rows)
+    stores += start(sems, heads, (q_out, saved[1]), (k_out, saved[2]), (v_out, saved[3]), (aux, saved[4]))
+    finish(stores)
+
+
+def embed_kernel(ids, att, wpt_own, wpt_other, xp_own, xp_other, out, wpt, wpt_held, xp, sems):
+    load = start(sems, 0, (xp_own, xp))
+    total = (wpt_own[...].astype(F32) + wpt_other[...].astype(F32)).astype(BF16)
+    wpt_held[...] = total
+    store = start(sems, 1, (wpt_held, wpt))
+    part = dot_nt(att[...], total) + xp_other[...].astype(F32)
+    finish(load)
+    out[...] = (part + xp[...]).astype(BF16).reshape(out.shape)
+    finish(store)
+
+
+def sum_kernel(ids, parts, out):
+    total = jnp.sum(parts[...].astype(F32), axis=0).astype(BF16)
+    for at in range(out.shape[0]):
+        out[at] = total
 
 
 def feature_parts(rows, gm, glayer, x_rows, centre, inverse, held, m, store):
@@ -186,18 +240,23 @@
     store(slice(half, half + 128), lanes((total, total_dot), rows).astype(BF16))
 
 
-def encoder_back_kernel(
-    ids, g_own, g_other, wpt, e_in, q_in, k_in, v_in, aux, x_in, w, we, first, gmix, glayer_out, few, held, sems
-):
-    copies = fetch(w, held, sems)
-    rows = q_in.shape[0]
-    width = q_in.shape[1]
+def encoder_back_kernel(ids, g_own, g_other, we, *refs):
+    sources = refs[:7]
+    w = refs[7]
+    right, left, gmix_out, glayer_out = refs[8:12]
+    wpt, e_in, q_in, k_in, v_in, aux, x_in, held, gmix, glayer, few, sems = refs[12:]
+    loads = start(sems, 0, *zip(sources, (wpt, e_in, q_in, k_in, v_in, aux, x_in)))
+    w_loads = start(sems, 7, *[(w.at[at], held.at[at]) for at in range(3)])
+    rows, width = q_in.shape
     heads = width // HD
     tok = x_in.shape[2]
     group = 8 * tok
     m = ids[1]
     factor = HD**-0.5
     gemb = jnp.concatenate([g_own[...], g_other[...]])
+    glayer[...] = dot_nt(gemb, we[...])
+    stores = start(sems, 10, (glayer, glayer_out))
+    finish(loads)
     gatt = dot(gemb, wpt[...]).astype(BF16)
     for head in range(heads):
         cols = slice(head * HD, (head + 1) * HD)
@@ -216,7 +275,7 @@
         gmix[:, head * HD : (head + 1) * HD] = norm_back(q_hat, q_inv, gq).astype(BF16)
         gmix[:, width + head * HD : width + (head + 1) * HD] = norm_back(k_hat, k_inv, gk).astype(BF16)
         gmix[:, 2 * width + head * HD : 2 * width + (head + 1) * HD] = gv.astype(BF16)
-    glayer_out[...] = dot_nt(gemb, we[...])
+    stores += start(sems, 11, (gmix, gmix_out))
     ats = [lax.rem(m + 4, 8), lax.rem(m + 5, 8)]
     blocks = [(rel, at) for at in ats for rel in range(2)]
 
@@ -232,15 +291,19 @@
         return jnp.concatenate([x_in[rel, at, :, cols] for rel, at in blocks])
 
     def store(cols, value):
-        first[:, cols] = value
-
-    for copy in copies:
-        copy.wait()
-    feature_parts(4 * tok, few[...], rows_of(glayer_out), x_rows, some[:, 0:1], some[:, 1:2], held, m, store)
-
-
-def feature_kernel(ids, gmix, glayer, aux, x_in, w, out, held, sems):
-    copies = fetch(w, held, sems)
+        right[:, cols] = value[: 2 * tok]
+        left[:, cols] = value[2 * tok :]
+
+    finish(w_loads)
+    feature_parts(4 * tok, few[...], rows_of(glayer), x_rows, some[:, 0:1], some[:, 1:2], held, m, store)
+    finish(stores)
+
+
+def feature_kernel(ids, *refs):
+    sources, w, out = refs[:4], refs[4], refs[5]
+    gmix, glayer, aux, x_in, held, sems = refs[6:]
+    loads = start(sems, 0, *zip(sources, (gmix, glayer, aux, x_in)))
+    loads += start(sems, 4, *[(w.at[at], held.at[at]) for at in range(3)])
     tok = x_in.shape[2]
     rows = gmix.shape[0]
 
@@ -252,8 +315,7 @@
         out[:, :tok, cols] = value[0]
         out[:, tok:, cols] = value[1]
 
-    for copy in copies:
-        copy.wait()
+    finish(loads)
     feature_parts(rows, gmix[...], glayer[...], x_rows, aux[:, 0:1], aux[:, 1:2], held, ids[1], store)
 
 
@@ -285,7 +347,11 @@
     return back.reshape(width, n)
 
 
-def mask_kernel(ids, table, mask, w, pos_vis, vis_row, hidden, k_t, v, wq_t, wk_t):
+def mask_kernel(ids, table_in, mask, w, pos_vis, vis_row, hidden, k_t, v, wq_t, wk_t, table, sems):
+    load = start(sems, 0, (table_in, table))
+    wq_t[...] = w[0].T
+    wk_t[...] = w[1].T
+    finish(load)
     members, pos_dev = table.shape[0], table.shape[1] - 16
     npos, width = members * pos_dev, table.shape[2]
     nvis = vis_row.shape[1]
@@ -300,8 +366,6 @@
     hidden[...] = 1.0 - dot_nt(jnp.ones((16, nvis), BF16), hot)[0:1, :]
     hat, _ = row_norm(pos_all.astype(F32) + mask[...].astype(F32))
     low = hat.astype(BF16)
-    wq_t[...] = w[0].T
-    wk_t[...] = w[1].T
     key_hat, _ = head_norm_t(dot_nt(wk_t[...], low))
     k_t[...] = key_hat.astype(BF16)
     v[...] = dot(low, w[2]).astype(BF16)
@@ -427,16 +491,12 @@
     def exchange(value, axis):
         return lax.all_to_all(value, axis, 0, 0, tiled=True)
 
-    spread = 4 if copies % 4 == 0 else 1
-    dec_cols = dec_width // spread
-    place = lax.axis_index("dp") % spread
-    pieces = lax.all_gather(
-        lax.dynamic_slice_in_dim(embed_weight, place * dec_cols, dec_cols, 1).T, "mp", axis=0, tiled=False
-    )
-
     mine = lax.dynamic_slice_in_dim(x_own, section * half, half, 1)
     theirs = swap(lax.dynamic_slice_in_dim(x_own, (1 - section) * half, half, 1))
-    chunk = jnp.concatenate([mine, theirs])
+    dec_cols = dec_width // copies
+    we_t = lax.dynamic_slice_in_dim(embed_weight, lax.axis_index("dp") * dec_cols, dec_cols, 1).T
+    we_t = we_t.reshape(dec_cols // 32, 32, slab).transpose(1, 0, 2).reshape(32, -1)
+    chunk = jnp.concatenate([jnp.concatenate([mine, theirs]), we_t], axis=1)
     chunks = {0: chunk}
     right = left = chunk
     for step in range(1, 5):
@@ -446,7 +506,7 @@
             left = shift(left, -1)
             chunks[step] = left
 
-    index, _, _ = lax.optimization_barrier((vis_index[0], chunks[-1], pieces))
+    index, _ = lax.optimization_barrier((vis_index[0], chunks[-1]))
     row = jnp.zeros((nvis,), jnp.int32)
     row = lax.dynamic_update_slice_in_dim(row, index, member * tok, 0)
     codes = jnp.pad(jnp.stack([row // 32, row % 32]), ((0, 14), (0, dec_width - nvis)))
@@ -454,62 +514,80 @@
     table = lax.all_gather(table, ("section", "mp"), axis=0, tiled=False)
 
     w_in = input_weight.transpose(1, 0, 2)
-    held = (pltpu.VMEM(w_in.shape, BF16), pltpu.SemaphoreType.DMA((3,)))
-    wp_part, wp_send = call(
-        fold_kernel, (sds((dec_cols, width), F32), sds((dec_cols, width), BF16)), ids, pieces, output_weight
-    )
-    x_all, p_own, p_send, stats, xp_own, xp_send = call(
+    held = sds(w_in.shape, BF16)
+    ordered = [chunks[offset] for offset in OFFSETS]
+    (wp_part,) = call(
+        fold_kernel,
+        [sds((copies, dec_cols, width), BF16)],
+        ids,
+        *ordered,
+        output_weight,
+        scratch=[sds((dec_cols, half), BF16)],
+    )
+    wpt_own = exchange(wp_part, "dp").reshape(dec_width, width)
+    ids_late, _ = lax.optimization_barrier((ids, wp_part))
+    x_all, p_own, p_send, xp_own, xp_send = call(
         project_kernel,
-        (
+        [
             sds((2, 8, tok, half), BF16),
-            sds((nvis + 16, 3 * width), F32),
-            sds((nvis + 16, 3 * width), BF16),
-            sds((nvis, 128), F32),
+            sds((nvis + 16, 3 * width + 128), F32),
+            sds((nvis + 16, 3 * width + 128), BF16),
             sds((group, dec_width), F32),
             sds((group, dec_width), BF16),
-        ),
-        ids,
-        *[chunks[offset] for offset in OFFSETS],
+        ],
+        ids_late,
+        *ordered,
         w_in,
         embed_weight,
-        scratch=(pltpu.VMEM((nvis + 16, half), BF16),) + held,
+        scratch=[
+            sds((2, 8, tok, half), BF16),
+            sds((nvis + 16, half), BF16),
+            held,
+            sds((group, dec_width), F32),
+        ],
         far=(9,),
+        far_out=(0, 3),
+        copies=5,
+        limit=28,
     )
     p_other = swap(p_send)
-    stats_other = swap(stats)
-    wp_piece = (wp_part + swap(wp_send).astype(F32)).astype(BF16)
-    wpt = lax.all_to_all(
-        jnp.broadcast_to(wp_piece, (spread, dec_cols, width)),
-        "dp",
-        0,
-        0,
-        tiled=True,
-        axis_index_groups=[[y * spread + x for x in range(spread)] for y in range(copies // spread)],
-    ).reshape(dec_width, width)
+    wpt_other = swap(wpt_own)
     xp_other = swap(xp_send)
-
+    saved = [
+        sds((heads, nvis, nvis), BF16),
+        sds((nvis, width), F32),
+        sds((nvis, width), F32),
+        sds((nvis, width), BF16),
+        sds((nvis, 128), F32),
+    ]
     att, e_enc, q_enc, k_enc, v_enc, aux = call(
         attend_kernel,
-        (
-            sds((group, width), BF16),
-            sds((heads, nvis, nvis), BF16),
-            sds((nvis, width), F32),
-            sds((nvis, width), F32),
-            sds((nvis, width), BF16),
-            sds((nvis, 128), F32),
-        ),
+        [sds((group, width), BF16)] + saved,
         ids,
         p_own,
         p_other,
-        stats,
-        stats_other,
-    )
-    embed_part = dot_nt(att, wpt) + xp_own + xp_other.astype(F32)
+        scratch=saved,
+        far_out=(1, 2, 3, 4, 5),
+        copies=heads + 4,
+    )
+    embed_part, wpt = call(
+        embed_kernel,
+        [sds((8, tok, dec_width), BF16), sds((dec_width, width), BF16)],
+        ids,
+        att,
+        wpt_own,
+        wpt_other,
+        xp_own,
+        xp_other,
+        scratch=[sds((dec_width, width), BF16), sds((group, dec_width), F32)],
+        far=(4,),
+        far_out=(1,),
+        copies=2,
+    )
 
     def reduce_and_gather(part):
-        received = exchange(part.astype(BF16).reshape(8, tok, dec_width), "mp")
-        total = jnp.sum(received.astype(F32), axis=0).astype(BF16)
-        gathered = exchange(jnp.broadcast_to(total, (8, tok, dec_width)), "mp").reshape(group, dec_width)
+        (total,) = call(sum_kernel, [sds((8, tok, dec_width), BF16)], ids, exchange(part, "mp"))
+        gathered = exchange(total, "mp").reshape(group, dec_width)
         return gathered, swap(gathered)
 
     w_dec = decoder_input.transpose(1, 0, 2)
@@ -517,7 +595,7 @@
     table, embed_part = lax.optimization_barrier((table, embed_part))
     pos_vis, vis_row, hidden, km_t, vm, wq_t, wk_t = call(
         mask_kernel,
-        (
+        [
             sds((nvis, dec_width), F32),
             sds((1, nvis), jnp.int32),
             sds((1, npos), F32),
@@ -525,11 +603,14 @@
             sds((npos, dec_width), BF16),
             sds((dec_width, dec_width), BF16),
             sds((dec_width, dec_width), BF16),
-        ),
+        ],
         ids,
         table,
         mask_row,
         w_dec,
+        scratch=[sds(table.shape, BF16)],
+        far=(1,),
+        copies=1,
     )
     emb_own, emb_other = reduce_and_gather(embed_part)
 
@@ -537,11 +618,11 @@
     rows = (128 // DHD) * pos_dev
     prediction, g_own, g_send = call(
         decoder_kernel,
-        (
+        [
             sds((pos_dev, target.shape[2]), BF16),
             sds((group, dec_width), F32),
             sds((group, dec_width), BF16),
-        ),
+        ],
         ids,
         vis_row,
         emb_own,
@@ -558,20 +639,23 @@
         decoder_output,
         pixel_weight,
         target[0],
-        scratch=(pltpu.VMEM((groups, rows, npos), BF16), pltpu.VMEM((groups, rows, nvis), BF16)),
-    )
-    ge_own, ge_other = reduce_and_gather(g_own + swap(g_send).astype(F32))
-
-    first, gmix, glayer = call(
+        scratch=[sds((groups, rows, npos), BF16), sds((groups, rows, nvis), BF16)],
+    )
+    g_part = (g_own + swap(g_send).astype(F32)).astype(BF16)
+    ge_own, ge_other = reduce_and_gather(g_part.reshape(8, tok, dec_width))
+
+    right, left, gmix, glayer = call(
         encoder_back_kernel,
-        (
-            sds((4 * tok, half + 128), BF16),
+        [
+            sds((2 * tok, half + 128), BF16),
+            sds((2 * tok, half + 128), BF16),
             sds((nvis, 3 * width), BF16),
             sds((nvis, slab), F32),
-        ),
+        ],
         ids,
         ge_own,
         ge_other,
+        embed_weight,
         wpt,
         e_enc,
         q_enc,
@@ -580,36 +664,46 @@
         aux,
         x_all,
         w_in,
-        embed_weight,
-        scratch=(pltpu.VMEM((4 * tok, 3 * width), BF16),) + held,
-        far=(10,),
-    )
-    parts = call(
+        scratch=[sds((dec_width, width), BF16)]
+        + saved
+        + [sds(x_all.shape, BF16), held, sds((nvis, 3 * width), BF16), sds((nvis, slab), F32)]
+        + [sds((4 * tok, 3 * width), BF16)],
+        far=tuple(range(4, 12)),
+        far_out=(2, 3),
+        copies=12,
+    )
+    (parts,) = call(
         feature_kernel,
-        sds((8, 2 * tok, half + 128), BF16),
+        [sds((8, 2 * tok, half + 128), BF16)],
         ids,
         gmix,
         glayer,
         aux,
         x_all,
         w_in,
-        scratch=held,
-        far=(5,),
+        scratch=[
+            sds((nvis, 3 * width), BF16),
+            sds((nvis, slab), F32),
+            sds((nvis, 128), F32),
+            sds(x_all.shape, BF16),
+            held,
+        ],
+        far=(1, 2, 3, 4, 5),
+        copies=7,
     )
 
     def part(offset):
         return lax.dynamic_index_in_dim(parts, (column + offset) % 8, 0, False).astype(F32)
 
-    right, left = first[: 2 * tok], first[2 * tok :]
     for step in range(3):
         moved_right, moved_left = shift(right, 1), shift(left, -1)
         right = (moved_right.astype(F32) + part(3 - step)).astype(BF16)
         if step < 2:
             left = (moved_left.astype(F32) + part(-2 + step)).astype(BF16)
     total = shift(right, 1).astype(F32) + moved_left.astype(F32) + part(0)
-    patch_grad = call(
+    (patch_grad,) = call(
         final_kernel,
-        sds((tok, model), BF16),
+        [sds((tok, model), BF16)],
         ids,
         total[:tok],
         swap(total[tok:].astype(BF16)),

time: 248 us -> 231 us (0.931)
  blocking collectives: 72.8 us -> 52.8 us
  starting transfers between devices: 58.9 us -> 41.8 us
  waiting for transfers between devices: 25.7 us -> 42.2 us
  Pallas kernels: 32.3 us -> 40.3 us
  other arithmetic: 6.28 us -> 1.96 us
    all_gather x1 -> x0, blocking collectives: 28 us -> none  [shards(): lax.all_gather(lax.dynamic_slice_in_dim(embed_weight, place * dec_cols, d...]
    ppermute x9 -> x8, starting transfers between devices: 40.9 us -> 20.4 us  [swap(): return lax.ppermute(value, 'section', [(0, 1), (1, 0)])]
    ppermute x14, waiting for transfers between devices: 21 us -> 37.7 us  [shift(): return lax.ppermute(value, 'mp', [(i, (i + by) % 8) for i in range(8)])]
    pallas_call x8 -> x11, Pallas kernels: 32.3 us -> 40.3 us  [call(): pl.pallas_call(kernel, out_shape=tuple(outs), in_specs=specs, out_specs=t...]
    all_to_all x4, blocking collectives: 44.8 us -> 52.8 us  [exchange(): return lax.all_to_all(value, axis, 0, 0, tiled=True)]
    unnamed x76 -> x87, local copies, waits for them, and re-layouts: 25.8 us -> 29.8 us
    all_to_all x1, starting transfers between devices: 4.01 us -> 6.73 us  [exchange(): return lax.all_to_all(value, axis, 0, 0, tiled=True)]
  transfers between devices with their start and end apart: 25 -> 24, of which waited for: 10 -> 12; matrix products, arithmetic and copies ran while one was open for 3% -> 1% of each run, Pallas kernels for 7% -> 10%
where the time goes in v1:
time: 231 us; the launch traced here: 226 us
  blocking collectives  52.8 us (23%)
  waiting for transfers between devices  42.2 us (18%)
  starting transfers between devices  41.8 us (18%)
  Pallas kernels  40.3 us (17%)
  local copies, waits for them, and re-layouts  32.6 us (14%)
  between operations  14.7 us (6%)
    all_to_all x4, blocking collectives, exchange(): return lax.all_to_all(value, axis, 0, 0, tiled=True)  52.8 us
    pallas_call x11, Pallas kernels, call(): pl.pallas_call(kernel, out_shape=tuple(outs), in_specs=specs, out_specs=t...  40.3 us
    ppermute x14, waiting for transfers between devices, shift(): return lax.ppermute(value, 'mp', [(i, (i + by) % 8) for i in range(8)])  37.7 us
    unnamed x87, local copies, waits for them, and re-layouts  29.8 us
    ppermute x8, starting transfers between devices, swap(): return lax.ppermute(value, 'section', [(0, 1), (1, 0)])  20.4 us
    ppermute x14, starting transfers between devices, shift(): return lax.ppermute(value, 'mp', [(i, (i + by) % 8) for i in range(8)])  14.6 us
    all_to_all x1, starting transfers between devices, exchange(): return lax.all_to_all(value, axis, 0, 0, tiled=True)  6.73 us
  transfers between devices with their start and end apart: 24, of which 12 were waited for; matrix products, arithmetic and copies ran while one was open for 1% of the time, Pallas kernels for 10%

profile of v1, /device:TPU:1, one launch (start us, length us, event | category | flops | bytes accessed | tf_op | source)
XLA Modules:
  0.0 226.3 jit_solution(6845100911173344133)
XLA Ops:
  8.2 3.3 %collective-permute-start = (bf16[16,3072]{1,0:T(8,128)(2,1)S(1)}, bf16[16,3072]{1,0:T(8,128)(2,1)S(1)}, u32[]{:S(2)}, u32[]{:S(2)}) collective-permute-start(bf16[16,3072]{1,0:T(8,128)(2,1)S(1)} %get-tuple-element.69), channel_id=1, source_target_pairs={{0,128},{128,0},{1,129},{129,1},{2,130},{130,2},{3,131},{131,3},{4... | collective-permute-start | bytes 294920 | tf_op jit(solution)/shard_map/ppermute | solution.py:486
  12.7 9.5 %collective-permute-done.1.refs_1_ = bf16[32,3456]{1,0:T(8,128)(2,1)S(1)} collective-permute-done((bf16[32,3456]{1,0:T(8,128)(2,1)S(1)}, bf16[32,3456]{1,0:T(8,128)(2,1)S(1)}, u32[]{:S(2)}, u32[]{:S(2)}) %collective-permute-start.1) | collective-permute-done | bytes 221216 | tf_op jit(solution)/shard_map/ppermute | solution.py:489
  26.2 4.8 %collective-permute-done.2.refs_2_ = bf16[32,3456]{1,0:T(8,128)(2,1)S(1)} collective-permute-done((bf16[32,3456]{1,0:T(8,128)(2,1)S(1)}, bf16[32,3456]{1,0:T(8,128)(2,1)S(1)}, u32[]{:S(2)}, u32[]{:S(2)}) %collective-permute-start.2) | collective-permute-done | bytes 221216 | tf_op jit(solution)/shard_map/ppermute | solution.py:489
  33.0 3.4 %collective-permute-done.4.refs_4_ = bf16[32,3456]{1,0:T(8,128)(2,1)S(1)} collective-permute-done((bf16[32,3456]{1,0:T(8,128)(2,1)S(1)}, bf16[32,3456]{1,0:T(8,128)(2,1)S(1)}, u32[]{:S(2)}, u32[]{:S(2)}) %collective-permute-start.4) | collective-permute-done | bytes 221216 | tf_op jit(solution)/shard_map/ppermute | solution.py:489
  39.1 3.5 %collective-permute-done.6.refs_6_ = bf16[32,3456]{1,0:T(8,128)(2,1)S(1)} collective-permute-done((bf16[32,3456]{1,0:T(8,128)(2,1)S(1)}, bf16[32,3456]{1,0:T(8,128)(2,1)S(1)}, u32[]{:S(2)}, u32[]{:S(2)}) %collective-permute-start.6) | collective-permute-done | bytes 221216 | tf_op jit(solution)/shard_map/ppermute | solution.py:489
  42.5 3.5 %collective-permute-done.7.refs_7_ = bf16[32,3456]{1,0:T(8,128)(2,1)S(1)} collective-permute-done((bf16[32,3456]{1,0:T(8,128)(2,1)S(1)}, bf16[32,3456]{1,0:T(8,128)(2,1)S(1)}, u32[]{:S(2)}, u32[]{:S(2)}) %collective-permute-start.7) | collective-permute-done | bytes 221216 | tf_op jit(solution)/shard_map/ppermute | solution.py:489
  51.9 6.7 %all-to-all-start = ((bf16[16,32,384]{2,1,0:T(8,128)(2,1)}), bf16[16,32,384]{2,1,0:T(8,128)(2,1)S(1)}, u32[]{:S(2)}, u32[]{:S(2)}) async-start(bf16[16,32,384]{2,1,0:T(8,128)(2,1)} %shard_map.122), calls=%async_computation | async-start | bytes 786432 | tf_op jit(solution)/shard_map/all_to_all | solution.py:492
  64.4 6.3 %shard_map.123 = (bf16[2,8,16,3072]{3,2,1,0:T(8,128)(2,1)S(1)}, f32[272,1280]{1,0:T(8,128)S(1)}, bf16[272,1280]{1,0:T(8,128)(2,1)}, f32[128,512]{1,0:T(8,128)S(1)}, bf16[128,512]{1,0:T(8,128)(2,1)S(1)}) custom-call(s32[3]{0:T(128)S(1)} %pad_add_fusion.ids, bf16[32,3456]{1,0:T(8,128)(2,1)S(1)} %pad_maximum_fusion.refs_0_, ...), custom_call_target="tpu_custom_call" | custom-call | tf_op jit(solution)/shard_map/pallas_call | solution.py:63
  72.7 6.4 %collective-permute-start.8 = (bf16[272,1280]{1,0:T(8,128)(2,1)}, bf16[272,1280]{1,0:T(8,128)(2,1)S(1)}, u32[]{:S(2)}, u32[]{:S(2)}) collective-permute-start(bf16[272,1280]{1,0:T(8,128)(2,1)} %get-tuple-element.36), channel_id=1, source_target_pairs={{0,128},{128,0},{1,129},{129,1},{2,130},{130,2},{3,131},{131,3},{4... | collective-permute-start | bytes 2088968 | tf_op jit(solution)/shard_map/ppermute | solution.py:486
  81.0 3.9 %shard_map.124 = (bf16[128,384]{1,0:T(8,128)(2,1)S(1)}, bf16[3,256,256]{2,1,0:T(8,128)(2,1)S(1)}, f32[256,384]{1,0:T(8,128)S(1)}, f32[256,384]{1,0:T(8,128)S(1)}...) custom-call(s32[3]{0:T(128)S(1)} %pad_add_fusion.ids, f32[272,1280]{1,0:T(8,128)S(1)} %get-tuple-element.35.p_own, ...), custom_call_target="tpu_custom_call" | custom-call | tf_op jit(solution)/shard_map/pallas_call | solution.py:63
  90.8 10.8 %all_to_all.25.parts = bf16[8,16,512]{2,1,0:T(8,128)(2,1)S(1)} all-to-all(bf16[8,16,512]{2,1,0:T(8,128)(2,1)S(1)} %get-tuple-element.43), channel_id=1, replica_groups=mesh['section'=2,'mp'=8,'dp'=16] {'mp'}, dimensions={0} | all-to-all | bytes 262144 | tf_op jit(solution)/shard_map/all_to_all | solution.py:492
  102.2 10.4 %all_to_all.26 = bf16[8,16,512]{2,1,0:T(8,128)(2,1)S(1)} all-to-all(bf16[8,16,512]{2,1,0:T(8,128)(2,1)S(1)} %shard_map.127), channel_id=1, replica_groups=mesh['section'=2,'mp'=8,'dp'=16] {'mp'}, dimensions={0} | all-to-all | bytes 262144 | tf_op jit(solution)/shard_map/all_to_all | solution.py:492
  112.6 3.2 %collective-permute-start.11 = (bf16[128,512]{1,0:T(8,128)(2,1)S(1)}, bf16[128,512]{1,0:T(8,128)(2,1)S(1)}, u32[]{:S(2)}, u32[]{:S(2)}) collective-permute-start(bf16[128,512]{1,0:T(8,128)(2,1)S(1)} %bitcast.51), channel_id=1, source_target_pairs={{0,128},{128,0},{1,129},{129,1},{2,130},{130,2},{3,131},{131,3},{4... | collective-permute-start | bytes 393224 | tf_op jit(solution)/shard_map/ppermute | solution.py:486
  118.6 3.0 %shard_map.126 = (f32[256,512]{1,0:T(8,128)S(1)}, s32[1,256]{1,0:T(1,128)S(1)}, f32[1,1024]{1,0:T(1,128)S(1)}, bf16[512,1024]{1,0:T(8,128)(2,1)S(1)}, bf16[1024,...) custom-call(s32[3]{0:T(128)S(1)} %pad_add_fusion.ids, ...), custom_call_target="tpu_custom_call" | custom-call | tf_op jit(solution)/shard_map/pallas_call | solution.py:63
  123.9 7.7 %shard_map.128 = (bf16[64,768]{1,0:T(8,128)(2,1)}, f32[128,512]{1,0:T(8,128)S(1)}, bf16[128,512]{1,0:T(8,128)(2,1)S(1)}) custom-call(s32[3]{0:T(128)S(1)} %pad_add_fusion.ids, s32[1,256]{1,0:T(1,128)S(1)} %get-tuple-element.42.vis_row, bf16[128,512]{1,0:T(8,128)(2,1)S(1)} %bitcast.52, bf16[128,512]{1,0:T(8,128)(2,1)S(1)} %collective-permute-done.11.emb_other, ...), custom_call_target="tpu_custom_call" | custom-call | tf_op jit(solution)/shard_map/pallas_call | solution.py:63
  133.0 11.0 %all_to_all.27.parts = bf16[8,16,512]{2,1,0:T(8,128)(2,1)S(1)} all-to-all(bf16[8,16,512]{2,1,0:T(8,128)(2,1)S(1)} %bitcast.54), channel_id=1, replica_groups=mesh['section'=2,'mp'=8,'dp'=16] {'mp'}, dimensions={0} | all-to-all | bytes 262144 | tf_op jit(solution)/shard_map/all_to_all | solution.py:492
  144.6 20.5 %all_to_all.28 = bf16[8,16,512]{2,1,0:T(8,128)(2,1)S(1)} all-to-all(bf16[8,16,512]{2,1,0:T(8,128)(2,1)S(1)} %shard_map.129), channel_id=1, replica_groups=mesh['section'=2,'mp'=8,'dp'=16] {'mp'}, dimensions={0} | all-to-all | bytes 262144 | tf_op jit(solution)/shard_map/all_to_all | solution.py:492
  168.6 8.1 %shard_map.130 = (bf16[32,3200]{1,0:T(8,128)(2,1)}, bf16[32,3200]{1,0:T(8,128)(2,1)S(1)}, bf16[256,1152]{1,0:T(8,128)(2,1)S(1)}, f32[256,384]{1,0:T(8,128)S(1)}) custom-call(s32[3]{0:T(128)S(1)} %pad_add_fusion.ids, bf16[128,512]{1,0:T(8,128)(2,1)S(1)} %bitcast.50, bf16[128,512]{1,0:T(8,128)(2,1)S(1)} %collective-permute-done.13.g_other, ...), custom_call_target="tpu_custom_call" | custom-call | tf_op jit(solution)/shard_map/pallas_call | solution.py:63
  181.6 3.0 %copy-done.1 = bf16[3072,3,384]{2,0,1:T(8,128)(2,1)S(1)} copy-done((bf16[3072,3,384]{2,0,1:T(8,128)(2,1)S(1)}, bf16[3072,3,384]{2,0,1:T(8,128)(2,1)}, u32[]{:S(2)}) %copy-start.1) | copy-done | bytes 7077912
  188.1 5.2 %shard_map.131 = bf16[8,32,3200]{2,1,0:T(8,128)(2,1)S(1)} custom-call(s32[3]{0:T(128)S(1)} %pad_add_fusion.ids, bf16[256,1152]{1,0:T(8,128)(2,1)S(1)} %copy-done.21, f32[256,384]{1,0:T(8,128)S(1)} %copy-done.32, f32[256,128]{1,0:T(8,128)S(1)} %get-tuple-element.58.refs_5_.refs_2_, bf16[2,8,16,3072]{3,2,1,0:T(8,128)(2,1)S(1)} %copy-done.6, ...), custom_call_target="tpu_custom_call" | custom-call | tf_op jit(solution)/shard_map/pallas_call | solution.py:63
  193.6 6.8 %collective-permute-done.15 = bf16[32,3200]{1,0:T(8,128)(2,1)S(1)} collective-permute-done((bf16[32,3200]{1,0:T(8,128)(2,1)S(1)}, bf16[32,3200]{1,0:T(8,128)(2,1)S(1)}, u32[]{:S(2)}, u32[]{:S(2)}) %collective-permute-start.15) | collective-permute-done | bytes 204832 | tf_op jit(solution)/shard_map/ppermute | solution.py:489
  203.2 3.1 %collective-permute-done.16 = bf16[32,3200]{1,0:T(8,128)(2,1)S(1)} collective-permute-done((bf16[32,3200]{1,0:T(8,128)(2,1)S(1)}, bf16[32,3200]{1,0:T(8,128)(2,1)S(1)}, u32[]{:S(2)}, u32[]{:S(2)}) %collective-permute-start.16) | collective-permute-done | bytes 204832 | tf_op jit(solution)/shard_map/ppermute | solution.py:489
  209.3 3.1 %collective-permute-done.17 = bf16[32,3200]{1,0:T(8,128)(2,1)S(1)} collective-permute-done((bf16[32,3200]{1,0:T(8,128)(2,1)S(1)}, bf16[32,3200]{1,0:T(8,128)(2,1)S(1)}, u32[]{:S(2)}, u32[]{:S(2)}) %collective-permute-start.17) | collective-permute-done | bytes 204832 | tf_op jit(solution)/shard_map/ppermute | solution.py:489
  212.5 4.2 %collective-permute-start.21 = (bf16[16,3200]{1,0:T(8,128)(2,1)S(1)}, bf16[16,3200]{1,0:T(8,128)(2,1)S(1)}, u32[]{:S(2)}, u32[]{:S(2)}) collective-permute-start(bf16[16,3200]{1,0:T(8,128)(2,1)S(1)} %slice.12), channel_id=1, source_target_pairs={{0,128},{128,0},{1,129},{129,1},{2,130},{130,2},{3,131},{131,3},{4... | collective-permute-start | bytes 307208 | tf_op jit(solution)/shard_map/ppermute | solution.py:486
  (147 shorter events, 60.0 us)
Async XLA Ops:
  7.2 83.7 %all-gather.3.cloned.1.call-start = ((), (), s32[]{:S(2)}) async-start(), calls=%async_computation.5 | async-start | bytes 1392640 | tf_op jit(solution)/shard_map/all_gather | solution.py:514
  8.2 4.4 %collective-permute-start = (bf16[16,3072]{1,0:T(8,128)(2,1)S(1)}, bf16[16,3072]{1,0:T(8,128)(2,1)S(1)}, u32[]{:S(2)}, u32[]{:S(2)}) collective-permute-start(bf16[16,3072]{1,0:T(8,128)(2,1)S(1)} %get-tuple-element.69), channel_id=1, source_target_pairs={{0,128},{128,0},{1,129},{129,1},{2,130},{130,2},{3,131},{131,3},{4... | collective-permute-start | bytes 294920 | tf_op jit(solution)/shard_map/ppermute | solution.py:486
  12.6 9.6 %collective-permute-start.1 = (bf16[32,3456]{1,0:T(8,128)(2,1)S(1)}, bf16[32,3456]{1,0:T(8,128)(2,1)S(1)}, u32[]{:S(2)}, u32[]{:S(2)}) collective-permute-start(bf16[32,3456]{1,0:T(8,128)(2,1)S(1)} %pad_maximum_fusion.refs_0_), channel_id=1, source_target_pairs={{0,16},{16,32},{32,48},{48,64},{64,80},{80,96},{96,112},{112,0},{1... | collective-permute-start | bytes 663560 | tf_op jit(solution)/shard_map/ppermute | solution.py:489
  24.6 6.4 %collective-permute-start.2 = (bf16[32,3456]{1,0:T(8,128)(2,1)S(1)}, bf16[32,3456]{1,0:T(8,128)(2,1)S(1)}, u32[]{:S(2)}, u32[]{:S(2)}) collective-permute-start(bf16[32,3456]{1,0:T(8,128)(2,1)S(1)} %pad_maximum_fusion.refs_0_), channel_id=1, source_target_pairs={{0,112},{16,0},{32,16},{48,32},{64,48},{80,64},{96,80},{112,96},{1... | collective-permute-start | bytes 663560 | tf_op jit(solution)/shard_map/ppermute | solution.py:489
  25.9 7.1 %collective-permute-start.3 = (bf16[32,3456]{1,0:T(8,128)(2,1)S(1)}, bf16[32,3456]{1,0:T(8,128)(2,1)S(1)}, u32[]{:S(2)}, u32[]{:S(2)}) collective-permute-start(bf16[32,3456]{1,0:T(8,128)(2,1)S(1)} %collective-permute-done.1.refs_1_), channel_id=1, source_target_pairs={{0,16},{16,32},{32,48},{48,64},{64,80},{80,96},{96,112},{112,0},{1... | collective-permute-start | bytes 663560 | tf_op jit(solution)/shard_map/ppermute | solution.py:489
  31.0 5.4 %collective-permute-start.4 = (bf16[32,3456]{1,0:T(8,128)(2,1)S(1)}, bf16[32,3456]{1,0:T(8,128)(2,1)S(1)}, u32[]{:S(2)}, u32[]{:S(2)}) collective-permute-start(bf16[32,3456]{1,0:T(8,128)(2,1)S(1)} %collective-permute-done.2.refs_2_), channel_id=1, source_target_pairs={{0,112},{16,0},{32,16},{48,32},{64,48},{80,64},{96,80},{112,96},{1... | collective-permute-start | bytes 663560 | tf_op jit(solution)/shard_map/ppermute | solution.py:489
  33.0 6.0 %collective-permute-start.5 = (bf16[32,3456]{1,0:T(8,128)(2,1)S(1)}, bf16[32,3456]{1,0:T(8,128)(2,1)S(1)}, u32[]{:S(2)}, u32[]{:S(2)}) collective-permute-start(bf16[32,3456]{1,0:T(8,128)(2,1)S(1)} %collective-permute-done.3.refs_3_), channel_id=1, source_target_pairs={{0,16},{16,32},{32,48},{48,64},{64,80},{80,96},{96,112},{112,0},{1... | collective-permute-start | bytes 663560 | tf_op jit(solution)/shard_map/ppermute | solution.py:489
  36.4 6.2 %collective-permute-start.6 = (bf16[32,3456]{1,0:T(8,128)(2,1)S(1)}, bf16[32,3456]{1,0:T(8,128)(2,1)S(1)}, u32[]{:S(2)}, u32[]{:S(2)}) collective-permute-start(bf16[32,3456]{1,0:T(8,128)(2,1)S(1)} %collective-permute-done.4.refs_4_), channel_id=1, source_target_pairs={{0,112},{16,0},{32,16},{48,32},{64,48},{80,64},{96,80},{112,96},{1... | collective-permute-start | bytes 663560 | tf_op jit(solution)/shard_map/ppermute | solution.py:489
  39.0 7.0 %collective-permute-start.7 = (bf16[32,3456]{1,0:T(8,128)(2,1)S(1)}, bf16[32,3456]{1,0:T(8,128)(2,1)S(1)}, u32[]{:S(2)}, u32[]{:S(2)}) collective-permute-start(bf16[32,3456]{1,0:T(8,128)(2,1)S(1)} %collective-permute-done.5.refs_5_), channel_id=1, source_target_pairs={{0,16},{16,32},{32,48},{48,64},{64,80},{80,96},{96,112},{112,0},{1... | collective-permute-start | bytes 663560 | tf_op jit(solution)/shard_map/ppermute | solution.py:489
  51.9 27.2 %all-to-all-start = ((bf16[16,32,384]{2,1,0:T(8,128)(2,1)}), bf16[16,32,384]{2,1,0:T(8,128)(2,1)S(1)}, u32[]{:S(2)}, u32[]{:S(2)}) async-start(bf16[16,32,384]{2,1,0:T(8,128)(2,1)} %shard_map.122), calls=%async_computation | async-start | bytes 786432 | tf_op jit(solution)/shard_map/all_to_all | solution.py:492
  72.7 8.4 %collective-permute-start.8 = (bf16[272,1280]{1,0:T(8,128)(2,1)}, bf16[272,1280]{1,0:T(8,128)(2,1)S(1)}, u32[]{:S(2)}, u32[]{:S(2)}) collective-permute-start(bf16[272,1280]{1,0:T(8,128)(2,1)} %get-tuple-element.36), channel_id=1, source_target_pairs={{0,128},{128,0},{1,129},{129,1},{2,130},{130,2},{3,131},{131,3},{4... | collective-permute-start | bytes 2088968 | tf_op jit(solution)/shard_map/ppermute | solution.py:486
  79.1 8.8 %collective-permute-start.9 = (bf16[512,384]{1,0:T(8,128)(2,1)S(1)}, bf16[512,384]{1,0:T(8,128)(2,1)S(1)}, u32[]{:S(2)}, u32[]{:S(2)}) collective-permute-start(bf16[512,384]{1,0:T(8,128)(2,1)S(1)} %bitcast.45), channel_id=1, source_target_pairs={{0,128},{128,0},{1,129},{129,1},{2,130},{130,2},{3,131},{131,3},{4... | collective-permute-start | bytes 1179656 | tf_op jit(solution)/shard_map/ppermute | solution.py:486
  79.2 8.7 %collective-permute-start.10 = (bf16[128,512]{1,0:T(8,128)(2,1)S(1)}, bf16[128,512]{1,0:T(8,128)(2,1)S(1)}, u32[]{:S(2)}, u32[]{:S(2)}) collective-permute-start(bf16[128,512]{1,0:T(8,128)(2,1)S(1)} %get-tuple-element.39), channel_id=1, source_target_pairs={{0,128},{128,0},{1,129},{129,1},{2,130},{130,2},{3,131},{131,3},{4... | collective-permute-start | bytes 393224 | tf_op jit(solution)/shard_map/ppermute | solution.py:486
  112.6 9.0 %collective-permute-start.11 = (bf16[128,512]{1,0:T(8,128)(2,1)S(1)}, bf16[128,512]{1,0:T(8,128)(2,1)S(1)}, u32[]{:S(2)}, u32[]{:S(2)}) collective-permute-start(bf16[128,512]{1,0:T(8,128)(2,1)S(1)} %bitcast.51), channel_id=1, source_target_pairs={{0,128},{128,0},{1,129},{129,1},{2,130},{130,2},{3,131},{131,3},{4... | collective-permute-start | bytes 393224 | tf_op jit(solution)/shard_map/ppermute | solution.py:486
  131.6 1.4 collective-permute-start.12
  165.1 3.4 %collective-permute-start.13 = (bf16[128,512]{1,0:T(8,128)(2,1)S(1)}, bf16[128,512]{1,0:T(8,128)(2,1)S(1)}, u32[]{:S(2)}, u32[]{:S(2)}) collective-permute-start(bf16[128,512]{1,0:T(8,128)(2,1)S(1)} %bitcast.49), channel_id=1, source_target_pairs={{0,128},{128,0},{1,129},{129,1},{2,130},{130,2},{3,131},{131,3},{4... | collective-permute-start | bytes 393224 | tf_op jit(solution)/shard_map/ppermute | solution.py:486
  178.9 14.4 %collective-permute-start.14 = (bf16[32,3200]{1,0:T(8,128)(2,1)}, bf16[32,3200]{1,0:T(8,128)(2,1)S(1)}, u32[]{:S(2)}, u32[]{:S(2)}) collective-permute-start(bf16[32,3200]{1,0:T(8,128)(2,1)} %get-tuple-element.60), channel_id=1, source_target_pairs={{0,16},{16,32},{32,48},{48,64},{64,80},{80,96},{96,112},{112,0},{1... | collective-permute-start | bytes 614408 | tf_op jit(solution)/shard_map/ppermute | solution.py:489
  179.2 14.3 %collective-permute-start.18 = (bf16[32,3200]{1,0:T(8,128)(2,1)}, bf16[32,3200]{1,0:T(8,128)(2,1)S(1)}, u32[]{:S(2)}, u32[]{:S(2)}) collective-permute-start(bf16[32,3200]{1,0:T(8,128)(2,1)} %copy-done.39), channel_id=1, source_target_pairs={{0,112},{16,0},{32,16},{48,32},{64,48},{80,64},{96,80},{112,96},{1... | collective-permute-start | bytes 614408 | tf_op jit(solution)/shard_map/ppermute | solution.py:489
  193.4 6.9 %collective-permute-start.15 = (bf16[32,3200]{1,0:T(8,128)(2,1)S(1)}, bf16[32,3200]{1,0:T(8,128)(2,1)S(1)}, u32[]{:S(2)}, u32[]{:S(2)}) collective-permute-start(bf16[32,3200]{1,0:T(8,128)(2,1)S(1)} %fusion.4), channel_id=1, source_target_pairs={{0,16},{16,32},{32,48},{48,64},{64,80},{80,96},{96,112},{112,0},{1... | collective-permute-start | bytes 614408 | tf_op jit(solution)/shard_map/ppermute | solution.py:489
  200.5 5.9 %collective-permute-start.16 = (bf16[32,3200]{1,0:T(8,128)(2,1)S(1)}, bf16[32,3200]{1,0:T(8,128)(2,1)S(1)}, u32[]{:S(2)}, u32[]{:S(2)}) collective-permute-start(bf16[32,3200]{1,0:T(8,128)(2,1)S(1)} %get-tuple-element.66), channel_id=1, source_target_pairs={{0,16},{16,32},{32,48},{48,64},{64,80},{80,96},{96,112},{112,0},{1... | collective-permute-start | bytes 614408 | tf_op jit(solution)/shard_map/ppermute | solution.py:489
  200.6 5.8 %collective-permute-start.19 = (bf16[32,3200]{1,0:T(8,128)(2,1)S(1)}, bf16[32,3200]{1,0:T(8,128)(2,1)S(1)}, u32[]{:S(2)}, u32[]{:S(2)}) collective-permute-start(bf16[32,3200]{1,0:T(8,128)(2,1)S(1)} %get-tuple-element.67), channel_id=1, source_target_pairs={{0,112},{16,0},{32,16},{48,32},{64,48},{80,64},{96,80},{112,96},{1... | collective-permute-start | bytes 614408 | tf_op jit(solution)/shard_map/ppermute | solution.py:489
  206.5 5.9 %collective-permute-start.17 = (bf16[32,3200]{1,0:T(8,128)(2,1)S(1)}, bf16[32,3200]{1,0:T(8,128)(2,1)S(1)}, u32[]{:S(2)}, u32[]{:S(2)}) collective-permute-start(bf16[32,3200]{1,0:T(8,128)(2,1)S(1)} %get-tuple-element.64), channel_id=1, source_target_pairs={{0,16},{16,32},{32,48},{48,64},{64,80},{80,96},{96,112},{112,0},{1... | collective-permute-start | bytes 614408 | tf_op jit(solution)/shard_map/ppermute | solution.py:489
  206.6 5.8 %collective-permute-start.20 = (bf16[32,3200]{1,0:T(8,128)(2,1)S(1)}, bf16[32,3200]{1,0:T(8,128)(2,1)S(1)}, u32[]{:S(2)}, u32[]{:S(2)}) collective-permute-start(bf16[32,3200]{1,0:T(8,128)(2,1)S(1)} %get-tuple-element.65), channel_id=1, source_target_pairs={{0,112},{16,0},{32,16},{48,32},{64,48},{80,64},{96,80},{112,96},{1... | collective-permute-start | bytes 614408 | tf_op jit(solution)/shard_map/ppermute | solution.py:489
  212.5 5.2 %collective-permute-start.21 = (bf16[16,3200]{1,0:T(8,128)(2,1)S(1)}, bf16[16,3200]{1,0:T(8,128)(2,1)S(1)}, u32[]{:S(2)}, u32[]{:S(2)}) collective-permute-start(bf16[16,3200]{1,0:T(8,128)(2,1)S(1)} %slice.12), channel_id=1, source_target_pairs={{0,128},{128,0},{1,129},{129,1},{2,130},{130,2},{3,131},{131,3},{4... | collective-permute-start | bytes 307208 | tf_op jit(solution)/shard_map/ppermute | solution.py:486
  (43 other events, 512.5 us)
Sparse Core Ops, SparseCore 0:
  24.8 39.6 all-gather.2
